TPU v7x, 256 devices: a whole 4x4x8 slice. The times are simulated.
256 devices in a mesh: lat: 8 (over y_lo, x), lon: 32 (over z, y_hi, core).
Axes of the slice: x: 4, y: 4 (y_hi: 2, y_lo: 2; y = y_hi * 2 + y_lo), z: 8, core: 2. Of those that a mesh axis runs over, the one named last changes fastest.
Arguments:
- signal: bfloat16 [64, 196608], P('lat', 'lon'), may hold values from -6 to 6
- cotangent: bfloat16 [64, 196608], P('lat', 'lon'), may hold values from -6 to 6
- qkv_weight: bfloat16 [2, 96, 288], replicated, may hold values from -0.625 to 0.625
- proj_weight: bfloat16 [2, 96, 96], replicated, may hold values from -0.625 to 0.625
- up_weight: bfloat16 [2, 96, 384], replicated, may hold values from -0.625 to 0.625
- down_weight: bfloat16 [2, 384, 96], replicated, may hold values from -0.3125 to 0.3125
- gdn_gamma: float32 [2, 96, 96], replicated, may hold values from 0.001 to 0.02
- gdn_beta: float32 [2, 96], replicated, may hold values from 0.25 to 4
- rel_table: float32 [2, 3, 225], replicated, may hold values from -3 to 250
Outputs:
- decoded: bfloat16 [64, 196608], P('lat', 'lon')
- signal_grad: bfloat16 [64, 196608], P('lat', 'lon')
- qkv_grad: float32 [2, 96, 288], replicated
- proj_grad: float32 [2, 96, 96], replicated
- up_grad: float32 [2, 96, 384], replicated
- down_grad: float32 [2, 384, 96], replicated
- gamma_grad: float32 [2, 96, 96], replicated
- beta_grad: float32 [2, 96], replicated
- table_grad: float32 [2, 3, 225], replicated
All inputs are finite; a program needn't handle non-finite values.
Results may differ from a plain program's by a relative error of at most 0.025.
Values may be sent and summed in bfloat16 or wider, within the bound.
A program may use at most 64 MiB of HBM per device.

v0:
```python
import math

import jax
import jax.numpy as jnp
from jax import lax
from jax.sharding import PartitionSpec as P

C = 96
HEADS = 3
WIN = 8
SHIFT = 4


def from_behind(block, axis, distance):
    devices = range(lax.axis_size(axis))
    route = [((i - distance) % len(devices), i) for i in devices]
    return lax.ppermute(block, axis, route)


def layer_normed(values_in):
    center = values_in - jnp.mean(values_in, axis=-1, keepdims=True)
    spread = jnp.mean(center * center, axis=-1, keepdims=True)
    return center * lax.rsqrt(spread + 1e-05)


def offset_table():
    places = jnp.arange(WIN * WIN, dtype=jnp.int32)
    across = places // WIN
    inside = places % WIN
    offset = (across[:, None] - across[None, :] + WIN - 1) * (2 * WIN - 1) + (
        inside[:, None] - inside[None, :] + WIN - 1
    )
    slot_ids = jnp.arange((2 * WIN - 1) ** 2, dtype=jnp.int32)
    return (offset.reshape(-1)[:, None] == slot_ids[None, :]).astype(jnp.float32)


def to_windows(grid_data):
    rows_in, cols_in, channels = grid_data.shape
    grid_data = grid_data.reshape(rows_in // WIN, WIN, cols_in // WIN, WIN, channels)
    return grid_data.transpose(0, 2, 1, 3, 4).reshape(-1, WIN * WIN, channels)


def from_windows(grid_data, rows_in, cols_in):
    channels = grid_data.shape[-1]
    grid_data = grid_data.reshape(rows_in // WIN, cols_in // WIN, WIN, WIN, channels)
    return grid_data.transpose(0, 2, 1, 3, 4).reshape(rows_in, cols_in, channels)


def swin_block(tile_in, params, region):
    qkv_weight, proj_weight, up_weight, down_weight, gdn_gamma, gdn_beta, rel_table = params
    rows_in, cols_in = (tile_in.shape[0], tile_in.shape[1])
    head_size = C // HEADS
    signal = tile_in.astype(jnp.float32)
    normed = to_windows(layer_normed(signal).astype(jnp.bfloat16)).reshape(-1, C)
    triple = jnp.dot(normed, qkv_weight, preferred_element_type=jnp.float32).astype(jnp.bfloat16)
    triple = triple.reshape(-1, WIN * WIN, 3, HEADS, head_size)
    scores = jnp.einsum(
        "nqhd,nkhd->nhqk", triple[:, :, 0], triple[:, :, 1], preferred_element_type=jnp.float32
    )
    scores = scores * head_size ** (-0.5)
    pos_bias = jnp.dot(rel_table, offset_table().T, precision=lax.Precision.HIGHEST).reshape(
        HEADS, WIN * WIN, WIN * WIN
    )
    labels = to_windows(jnp.broadcast_to(region[:, None, None], (rows_in, cols_in, 1)))[:, :, 0]
    allowed = labels[:, None, :, None] == labels[:, None, None, :]
    scores = jnp.where(allowed, scores + pos_bias[None], -1000000000.0)
    row_peak = lax.stop_gradient(jnp.max(scores, axis=-1, keepdims=True))
    exp_scores = jnp.exp(scores - row_peak)
    weights = (exp_scores / jnp.sum(exp_scores, axis=-1, keepdims=True)).astype(jnp.bfloat16)
    mixed_heads = jnp.einsum(
        "nhqk,nkhd->nqhd", weights, triple[:, :, 2], preferred_element_type=jnp.float32
    )
    mixed_heads = mixed_heads.astype(jnp.bfloat16).reshape(-1, C)
    attended = jnp.dot(mixed_heads, proj_weight, preferred_element_type=jnp.float32).reshape(
        -1, WIN * WIN, C
    )
    hidden = signal + from_windows(attended, rows_in, cols_in)
    flat_rows = hidden.reshape(-1, C)
    lifted = jax.nn.gelu(
        jnp.dot(
            layer_normed(flat_rows).astype(jnp.bfloat16),
            up_weight,
            preferred_element_type=jnp.float32,
        )
    ).astype(jnp.bfloat16)
    mixed_out = flat_rows + jnp.dot(lifted, down_weight, preferred_element_type=jnp.float32)
    gdn_power = gdn_beta + jnp.dot(
        mixed_out * mixed_out, gdn_gamma, precision=lax.Precision.HIGHEST
    )
    return (mixed_out * lax.rsqrt(gdn_power)).reshape(rows_in, cols_in, C).astype(jnp.bfloat16)


def unroll(rolled_data, strip_width):
    eastward = from_behind(rolled_data[:, :, -strip_width:], "lon", 1)
    rolled_data = jnp.concatenate([eastward, rolled_data[:, :, :-strip_width]], axis=2)
    southward = from_behind(rolled_data[:, -SHIFT:], "lat", 1)
    return jnp.concatenate([southward, rolled_data[:, :-SHIFT]], axis=1)


def per_device(
    signal,
    cotangent,
    qkv_weight,
    proj_weight,
    up_weight,
    down_weight,
    gdn_gamma,
    gdn_beta,
    rel_table,
):
    rows_in = signal.shape[0]
    row_length = signal.shape[1]
    cols_in = row_length // C
    strip_width = SHIFT * C
    params = (qkv_weight, proj_weight, up_weight, down_weight, gdn_gamma, gdn_beta, rel_table)
    first_params = tuple((member[0] for member in params))
    second = tuple((member[1] for member in params))
    flat_region = jnp.zeros((rows_in,), jnp.int32)
    sectioned, first_back = jax.vjp(
        lambda tile_in, weights: swin_block(tile_in, weights, flat_region),
        signal.reshape(rows_in, cols_in, C),
        first_params,
    )
    paired = jnp.stack([sectioned.reshape(rows_in, row_length), cotangent])
    southern = from_behind(paired[:, :SHIFT], "lat", -1)
    lowered = jnp.concatenate([paired[:, SHIFT:], southern], axis=1)
    beside = from_behind(lowered[:, :, :strip_width], "lon", -1)
    shifted = jnp.concatenate([lowered[:, :, strip_width:], beside], axis=2)
    band_index = lax.axis_index("lat")
    row_index = jnp.arange(rows_in, dtype=jnp.int32)
    region = ((band_index == lax.axis_size("lat") - 1) & (row_index >= rows_in - SHIFT)).astype(
        jnp.int32
    )
    rolled_out, second_back = jax.vjp(
        lambda tile_in, weights: swin_block(tile_in, weights, region),
        shifted[0].reshape(rows_in, cols_in, C),
        second,
    )
    rolled_grad, second_grads = second_back(shifted[1].reshape(rows_in, cols_in, C))
    decoded = unroll(rolled_out.reshape(1, rows_in, row_length), strip_width)[0]
    qkv_two, proj_two, up_two, down_two, gamma_two, beta_two, table_two = [
        member.astype(jnp.float32) for member in second_grads
    ]
    back_grad = unroll(rolled_grad.reshape(1, rows_in, row_length), strip_width)[0]
    input_grad, first_grads = first_back(back_grad.reshape(rows_in, cols_in, C))
    qkv_one, proj_one, up_one, down_one, gamma_one, beta_one, table_one = [
        member.astype(jnp.float32) for member in first_grads
    ]
    totals = lax.psum(
        (
            jnp.stack([qkv_one, qkv_two]),
            jnp.stack([proj_one, proj_two]),
            jnp.stack([up_one, up_two]),
            jnp.stack([down_one, down_two]),
            jnp.stack([gamma_one, gamma_two]),
            jnp.stack([beta_one, beta_two]),
            jnp.stack([table_one, table_two]),
        ),
        ("lat", "lon"),
    )
    grad_scale = 1.0 / math.sqrt(rows_in * lax.axis_size("lat") * cols_in * lax.axis_size("lon"))
    return (
        decoded,
        input_grad.reshape(rows_in, row_length),
        totals[0] * grad_scale,
        totals[1] * grad_scale,
        totals[2] * grad_scale,
        totals[3] * grad_scale,
        totals[4] * grad_scale,
        totals[5] * grad_scale,
        totals[6] * grad_scale,
    )


def solution(mesh):
    in_specs = (P("lat", "lon"), P("lat", "lon"), P(), P(), P(), P(), P(), P(), P())
    out_specs = (P("lat", "lon"), P("lat", "lon"), P(), P(), P(), P(), P(), P(), P())
    return jax.shard_map(
        per_device, mesh=mesh, in_specs=in_specs, out_specs=out_specs, check_vma=False
    )
```

profile of v0, /device:TPU:1, one launch (start us, length us, event | category | flops | bytes accessed | tf_op | source)
XLA Modules:
  0.0 470.3 jit_solution(522812729452571193)
XLA Ops:
  7.3 1.0 reshape.681
  8.3 1.0 reshape.682
  10.7 2.2 convolution_bitcast_fusion.1
  21.5 1.0 fusion.65
  22.9 4.4 collective-permute-start
  27.5 2.2 convolution_bitcast_fusion
  30.6 0.7 copy.313
  31.5 0.8 sub.270
  32.4 0.8 reshape.674
  33.9 1.2 collective-permute-start.1
  35.3 3.8 collective-permute-done.1
  39.1 0.7 fusion.97
  40.5 0.8 reshape.683
  44.2 0.7 fusion.181
  44.9 1.5 fusion.187
  47.0 1.1 fusion.24
  48.8 0.8 copy.361
  49.6 1.2 copy.315
  50.8 0.9 reshape.662
  51.7 1.2 fusion.172
  53.6 0.9 multiply_reduce_fusion.2
  54.5 0.7 copy.316
  55.2 1.8 reshape.686
  56.9 1.8 copy.322
  58.7 0.8 copy.317
  59.5 1.4 multiply_add_fusion
  60.9 1.6 multiply_convert_fusion.2
  62.5 0.8 copy.318
  63.3 1.0 copy.320
  64.3 1.2 fusion.107
  66.6 1.7 fusion.173
  68.3 1.0 convolution_bitcast_fusion.4
  69.6 1.0 fusion.36
  70.7 1.4 fusion.52
  72.3 1.3 multiply_reduce_fusion.7
  73.7 0.8 fusion.32
  74.8 0.8 reshape.664
  75.9 0.8 reshape.667
  76.8 1.3 fusion.25
  78.9 0.9 fusion.180
  82.1 0.9 fusion.34
  85.4 0.8 reshape.675
  86.2 1.0 copy.321
  88.0 1.0 copy.363
  89.2 2.0 fusion.40
  92.5 0.8 broadcast_in_dim.117
  93.5 1.0 fusion.73
  94.6 3.7 collective-permute-start.4
  98.6 1.6 collective-permute-done.4
  100.3 0.7 fusion.131
  101.1 4.5 collective-permute-done.5
  112.8 0.7 copy-done.12
  117.0 1.4 fusion.39
  118.4 80.0 %all-reduce.6 = (f32[2,96]{1,0:T(2,128)S(1)}, f32[2,3,225]{2,1,0:T(4,128)S(1)}) all-reduce(f32[2,96]{1,0:T(2,128)S(1)} %pad_maximum_fusion.7, f32[2,3,225]{2,1,0:T(4,128)S(1)} %pad_maximum_fusion.6), channel_id=1, replica_groups=mesh['lat'=8,'lon'=32] {'lat','lon'}, use_global_device_ids=true, to_apply=%region_29.30 | all-reduce | flops 1542 | bytes 12336 | tf_op jit(solution)/shard_map/psum | solution.py:149
  202.0 0.7 maximum_convert_fusion.2
  203.4 0.7 maximum_convert_fusion.1
  204.1 0.7 maximum_convert_fusion
  205.2 0.7 fusion.76
  205.9 1.4 fusion.99
  207.3 250.7 %all-reduce.10.cloned.1.call-done = (f32[2,96,288]{2,1,0:T(8,128)}, f32[2,96,96]{2,1,0:T(8,128)}, f32[2,96,384]{2,1,0:T(8,128)}, f32[2,384,96]{1,2,0:T(8,128)}, f32[2,96,96]{2,1,0:T(8,128)}) async-done(((f32[2,96,288]{2,1,0:T(8,128)}, f32[2,96,96]{2,1,0:T(8,128)}, f32[2,96,384]{2,1,0:T(8,128)}, f32[2,384,96]{1,2,0:T(8,128)}, f32[2,96,96]{2,1,0:T(8,128)}), (f32[2,96,288]{2,1,0:T(8,128)}, ...) | async-done | bytes 958480 | tf_op jit(solution)/shard_map/psum | solution.py:149
  458.0 1.8 broadcast_multiply_fusion.2
  459.8 1.5 broadcast_multiply_fusion.4
  462.0 0.7 broadcast_multiply_fusion.1
  462.7 0.7 broadcast_multiply_fusion
  (381 shorter events, 43.0 us)
Async XLA Ops:
  7.2 2.7 copy-start.1
  7.2 450.8 %all-reduce.10.cloned.1.call-start = ((), (), s32[]{:S(2)}) async-start(), calls=%async_computation | async-start | bytes 2162688 | tf_op jit(solution)/shard_map/psum | solution.py:149
  7.2 2.8 copy-start.92
  7.3 3.3 copy-start.90
  9.8 3.3 copy-start.77
  9.9 4.0 copy-start.40
  10.7 16.7 %copy-start.86 = (s32[4096]{0:T(1024)}, s32[4096]{0:T(1024)S(1)}, u32[]{:S(2)}) copy-start(s32[4096]{0:T(1024)S(1)} %add.242) | copy-start | bytes 49156
  13.0 2.4 copy-start.32
  16.8 13.0 %copy-start.70 = (f32[8,3,64]{2,1,0:T(4,128)}, f32[8,3,64]{2,1,0:T(4,128)S(1)}, u32[]{:S(2)}) copy-start(f32[8,3,64]{2,1,0:T(4,128)S(1)} %get-tuple-element.102) | copy-start | bytes 18436
  19.9 1.6 copy-start.81
  20.8 2.1 copy-start.68
  22.9 11.0 %collective-permute-start = (bf16[2,4,6144]{2,1,0:T(4,128)(2,1)S(1)}, bf16[2,4,6144]{2,1,0:T(4,128)(2,1)S(1)}, u32[]{:S(2)}, u32[]{:S(2)}) collective-permute-start(bf16[2,4,6144]{2,1,0:T(4,128)(2,1)S(1)} %get-tuple-element.84), channel_id=1, source_target_pairs={{32,0},{64,32},{96,64},{128,96},{160,128},{192,160},{224,192},{0,2... | collective-permute-start | bytes 294920 | tf_op jit(solution)/shard_map/ppermute | solution.py:17
  29.8 15.1 %copy-start.56 = (pred[8,64,64]{1,2,0:T(8,128)(4,1)}, pred[8,64,64]{1,2,0:T(8,128)(4,1)S(1)}, u32[]{:S(2)}) copy-start(pred[8,64,64]{1,2,0:T(8,128)(4,1)S(1)} %broadcast_compare_fusion) | copy-start | bytes 98308
  33.9 5.1 %collective-permute-start.1 = (bf16[2,8,384]{2,1,0:T(8,128)(2,1)S(1)}, bf16[2,8,384]{2,1,0:T(8,128)(2,1)S(1)}, u32[]{:S(2)}, u32[]{:S(2)}) collective-permute-start(bf16[2,8,384]{2,1,0:T(8,128)(2,1)S(1)} %pad_maximum_fusion.5), channel_id=1, source_target_pairs={{1,0},{2,1},{3,2},{4,3},{5,4},{6,5},{7,6},{8,7},{9,8},{10,9},{11,1... | collective-permute-start | bytes 36872 | tf_op jit(solution)/shard_map/ppermute | solution.py:17
  39.0 1.1 copy-start.74
  40.4 2.5 copy-start.79
  40.5 2.4 copy-start.44
  44.9 1.5 copy-start.13
  44.9 1.5 copy-start.15
  54.5 4.2 copy-start.7
  59.5 3.0 copy-start.8
  63.3 2.2 copy-start.21
  63.3 2.2 copy-start.22
  64.3 1.2 copy-start.96
  69.6 1.0 copy-start.62
  70.7 1.4 copy-start.66
  70.7 1.5 copy-start.64
  70.7 1.6 copy-start.35
  72.3 1.4 copy-start
  72.3 2.3 copy-start.63
  74.7 1.0 copy-start.60
  76.7 1.3 copy-start.30
  76.7 1.3 copy-start.31
  76.7 1.3 copy-start.73
  81.5 1.5 copy-start.33
  83.4 2.0 copy-start.20
  85.3 3.8 copy-start.87
  87.4 3.8 copy-start.51
  87.4 3.8 copy-start.65
  88.0 12.3 %collective-permute-start.2 = (bf16[1,8,384]{2,1,0:T(8,128)(2,1)}, bf16[1,8,384]{2,1,0:T(8,128)(2,1)}, u32[]{:S(2)}, u32[]{:S(2)}) collective-permute-start(bf16[1,8,384]{2,1,0:T(8,128)(2,1)} %slice.148), channel_id=1, source_target_pairs={{31,0},{0,1},{1,2},{2,3},{3,4},{4,5},{5,6},{6,7},{7,8},{8,9},{9,10... | collective-permute-start | bytes 18440 | tf_op jit(solution)/shard_map/ppermute | solution.py:17
  88.0 3.2 copy-start.45
  88.0 3.2 copy-start.47
  92.2 1.3 copy-start.27
  92.2 1.3 copy-start.75
  93.5 4.8 %copy-start.39 = (bf16[512,96]{0,1:T(8,128)(2,1)S(1)}, bf16[512,96]{0,1:T(8,128)(2,1)}, u32[]{:S(2)}) copy-start(bf16[512,96]{0,1:T(8,128)(2,1)} %reshape.675) | copy-start | bytes 294916
  94.6 5.6 %collective-permute-start.4 = (bf16[1,8,384]{2,1,0:T(8,128)(2,1)S(1)}, bf16[1,8,384]{2,1,0:T(8,128)(2,1)S(1)}, u32[]{:S(2)}, u32[]{:S(2)}) collective-permute-start(bf16[1,8,384]{2,1,0:T(8,128)(2,1)S(1)} %slice.152), channel_id=1, source_target_pairs={{31,0},{0,1},{1,2},{2,3},{3,4},{4,5},{5,6},{6,7},{7,8},{8,9},{9,10... | collective-permute-start | bytes 18440 | tf_op jit(solution)/shard_map/ppermute | solution.py:17
  98.5 7.4 %copy-start.18 = (f32[512,96]{0,1:T(8,128)S(1)}, f32[512,96]{0,1:T(8,128)}, u32[]{:S(2)}) copy-start(f32[512,96]{0,1:T(8,128)} %copy-done.17) | copy-start | bytes 589828
  98.6 7.4 %copy-start.19 = (f32[512,96]{0,1:T(8,128)S(1)}, f32[512,96]{0,1:T(8,128)}, u32[]{:S(2)}) copy-start(f32[512,96]{0,1:T(8,128)} %get-tuple-element.107) | copy-start | bytes 589828
  100.2 5.4 %collective-permute-start.5 = (bf16[1,4,6144]{2,1,0:T(4,128)(2,1)S(1)}, bf16[1,4,6144]{2,1,0:T(4,128)(2,1)S(1)}, u32[]{:S(2)}, u32[]{:S(2)}) collective-permute-start(bf16[1,4,6144]{2,1,0:T(4,128)(2,1)S(1)} %fusion.130), channel_id=1, source_target_pairs={{224,0},{0,32},{32,64},{64,96},{96,128},{128,160},{160,192},{192,2... | collective-permute-start | bytes 147464 | tf_op jit(solution)/shard_map/ppermute | solution.py:17
  101.0 104.9 %collective-permute-start.3 = (bf16[1,4,6144]{2,1,0:T(4,128)(2,1)S(1)}, bf16[1,4,6144]{2,1,0:T(4,128)(2,1)S(1)}, u32[]{:S(2)}, u32[]{:S(2)}) collective-permute-start(bf16[1,4,6144]{2,1,0:T(4,128)(2,1)S(1)} %fusion.131), channel_id=1, source_target_pairs={{224,0},{0,32},{32,64},{64,96},{96,128},{128,160},{160,192},{192,2... | collective-permute-start | bytes 147464 | tf_op jit(solution)/shard_map/ppermute | solution.py:17
  106.1 1.1 copy-start.25
  115.8 1.2 copy-start.88
  116.7 1.7 copy-start.93
  116.7 1.7 copy-start.91
  116.7 82.8 %copy-start.49 = (f32[8,8,8]{2,1,0:T(8,128)S(1)}, f32[8,8,8]{2,1,0:T(8,128)}, u32[]{:S(2)}) copy-start(f32[8,8,8]{2,1,0:T(8,128)} %copy-done.48) | copy-start | bytes 6148
  116.8 82.8 %copy-start.41 = (f32[8,8,8]{2,1,0:T(8,128)S(1)}, f32[8,8,8]{2,1,0:T(8,128)}, u32[]{:S(2)}) copy-start(f32[8,8,8]{2,1,0:T(8,128)} %copy-done.40) | copy-start | bytes 6148
  116.8 82.8 %copy-start.43 = (f32[8,8,8]{2,1,0:T(8,128)S(1)}, f32[8,8,8]{2,1,0:T(8,128)}, u32[]{:S(2)}) copy-start(f32[8,8,8]{2,1,0:T(8,128)} %copy-done.42) | copy-start | bytes 6148
  200.7 1.3 copy-start.69
  200.9 2.5 copy-start.54
  201.0 3.1 copy-start.55
  204.1 1.1 copy-start.26
  458.0 3.3 copy-start.67
  458.0 4.0 copy-start.53
  458.0 4.7 %copy-start.52 = (f32[2,384,96]{1,2,0:T(8,128)S(1)}, f32[2,384,96]{1,2,0:T(8,128)}, u32[]{:S(2)}) copy-start(f32[2,384,96]{1,2,0:T(8,128)} %get-tuple-element.68) | copy-start | bytes 884740
  (41 other events, 33.4 us)
Sparse Core Ops, SparseCore 0:
  205.0 252.9 all-reduce.9
where the time goes:
time: 472 us; the launch traced here: 470 us
  waiting for transfers between devices  261 us (55%)
  blocking collectives  80 us (17%)
  local copies, waits for them, and re-layouts  47 us (10%)
  matrix products  32 us (7%)
  other arithmetic  25.3 us (5%)
  between operations  15.9 us (3%)
  starting transfers between devices  9.59 us (2%)
    psum x1, waiting for transfers between devices, per_device(): lax.psum((jnp.stack([qkv_one, qkv_two]), jnp.stack([proj_one, proj_two]),...  251 us
    psum x1, blocking collectives, per_device(): lax.psum((jnp.stack([qkv_one, qkv_two]), jnp.stack([proj_one, proj_two]),...  80 us
    unnamed x197, local copies, waits for them, and re-layouts  14 us
    ppermute x6, waiting for transfers between devices, from_behind(): return lax.ppermute(block, axis, route)  9.91 us
    ppermute x6, starting transfers between devices, from_behind(): return lax.ppermute(block, axis, route)  9.55 us
  transfers between devices with their start and end apart: 7, of which 4 were waited for; matrix products, arithmetic and copies ran while one was open for 7% of the time, Pallas kernels for 0%

commit v1 on v0

v1 whole, which is shorter than its diff:
```python
import functools
import math

import jax
import jax.numpy as jnp
from jax import lax
from jax.experimental import pallas as pl
from jax.experimental.pallas import tpu as pltpu
from jax.sharding import PartitionSpec as P

C = 96
HEADS = 3
HEAD = 32
HID = 384
WIN = 8
RELS = 225
SLOTS = 256
PIX = 512
HALF = 256
UNIT = 16
WINDOWS = 8
TOKENS = 64
ROWS = 1024
TILE = 8
EPS = 1e-05
GELU_A = math.sqrt(2.0 / math.pi)
GELU_B = 0.044715
MESH = pl.DeviceIdType.MESH
F32 = jnp.float32
BF16 = jnp.bfloat16


def iota(shape, dim):
    return lax.broadcasted_iota(jnp.int32, shape, dim)


def dot(a, b, over=(1, 0)):
    return lax.dot_general(a, b, (((over[0],), (over[1],)), ((), ())), preferred_element_type=F32)


def dot_split(a, b):
    high = a.astype(BF16)
    rest = a - high.astype(F32)
    middle = rest.astype(BF16)
    low = (rest - middle.astype(F32)).astype(BF16)
    return dot(high, b) + dot(middle, b) + dot(low, b)


def row_mean(a):
    return jnp.sum(a, axis=-1, keepdims=True) * (1.0 / C)


def normalise(v):
    center = v - row_mean(v)
    scale = lax.rsqrt(row_mean(center * center) + EPS)
    return center * scale, scale


def norm_back(grad, hat, scale):
    return scale * (grad - row_mean(grad) - hat * row_mean(grad * hat))


def stack_heads(a):
    head_of = iota(a.shape, 1) // HEAD
    zero = jnp.zeros_like(a)
    return jnp.concatenate([jnp.where(head_of == h, a, zero) for h in range(HEADS)], axis=0)


def merge_heads(a):
    parts = [a[h * TOKENS : (h + 1) * TOKENS] for h in range(HEADS)]
    head_of = iota((TOKENS, C), 1) // HEAD
    return jnp.where(head_of == 0, parts[0], jnp.where(head_of == 1, parts[1], parts[2]))


def window(ref, w):
    step = TOKENS // 2
    upper = ref[w * step : (w + 1) * step, :]
    lower = ref[HALF + w * step : HALF + (w + 1) * step, :]
    return jnp.concatenate([upper, lower], axis=0)


def put_window(ref, w, value):
    step = TOKENS // 2
    ref[w * step : (w + 1) * step, :] = value[:step].astype(ref.dtype)
    ref[HALF + w * step : HALF + (w + 1) * step, :] = value[step:].astype(ref.dtype)


def unfold(src, dst):
    low = iota((WIN, C), 0) < 4
    for group in range(16):
        part = src[:, group * 4 * C : (group + 1) * 4 * C].astype(F32)
        for pair in range(2):
            one = part[:, (2 * pair) * C : (2 * pair + 1) * C]
            two = part[:, (2 * pair + 1) * C : (2 * pair + 2) * C]
            at = (group * 2 + pair) * 8
            dst[at : at + 8, :] = jnp.where(low, one, pltpu.roll(two, 4, 0)).astype(dst.dtype)
            dst[HALF + at : HALF + at + 8, :] = jnp.where(low, pltpu.roll(one, 4, 0), two).astype(dst.dtype)


def fold(value, dst):
    low = iota((WIN, C), 0) < 4
    for group in range(16):
        parts = []
        for pair in range(2):
            at = (group * 2 + pair) * 8
            upper = value[at : at + 8]
            lower = value[HALF + at : HALF + at + 8]
            parts.append(jnp.where(low, upper, pltpu.roll(lower, 4, 0)))
            parts.append(jnp.where(low, pltpu.roll(upper, 4, 0), lower))
        dst[:, group * 4 * C : (group + 1) * 4 * C] = jnp.concatenate(parts, axis=1).astype(dst.dtype)


def rel_slots():
    entry = iota((RELS, SLOTS), 0)
    slot = iota((RELS, SLOTS), 1)
    return ((entry // 15 == slot % 16) & (entry % 15 == slot // 16)).astype(F32)


def spread_queries():
    query = iota((HEADS * TOKENS, HEADS * 128), 0)
    place = iota((HEADS * TOKENS, HEADS * 128), 1)
    inside = query % TOKENS
    row = (inside // 32) * 4 + inside % 4
    column = (inside % 32) // 4
    return ((query // TOKENS) * 128 + column * 16 + row == place).astype(F32)


def build_bias(table, bias):
    slots = dot_split(table, rel_slots().astype(BF16))
    sub = iota((8, SLOTS), 0)
    heads = []
    for h in range(HEADS):
        line = jnp.broadcast_to(slots[h : h + 1], (8, SLOTS))
        skew = line
        for s in range(1, 8):
            skew = jnp.where(sub == s, pltpu.roll(line, 16 * (s // 4) + s % 4, 1), skew)
        groups = []
        for g in range(8):
            turn = SLOTS - 119 + 32 * (g % 4) + 4 * (g // 4)
            groups.append(pltpu.roll(skew, turn % SLOTS, 1)[:, :128])
        heads.append(jnp.concatenate(groups, axis=0))
    wide = jnp.concatenate(heads, axis=1)
    back = spread_queries().astype(BF16)
    high = wide.astype(BF16)
    rest = wide - high.astype(F32)
    middle = rest.astype(BF16)
    low = (rest - middle.astype(F32)).astype(BF16)
    bias[...] = dot(high, back, (1, 1)) + dot(middle, back, (1, 1)) + dot(low, back, (1, 1))


def table_slots(total):
    wide = dot(total.astype(BF16), spread_queries().astype(BF16))
    sub = iota((8, SLOTS), 0)
    blank = jnp.zeros((8, 128), F32)
    lines = []
    for h in range(HEADS):
        skew = jnp.zeros((8, SLOTS), F32)
        for g in range(8):
            part = jnp.concatenate([wide[8 * g : 8 * g + 8, 128 * h : 128 * h + 128], blank], axis=1)
            skew = skew + pltpu.roll(part, 119 - 32 * (g % 4) - 4 * (g // 4), 1)
        line = skew
        for s in range(1, 8):
            line = jnp.where(sub == s, pltpu.roll(skew, SLOTS - 16 * (s // 4) - s % 4, 1), line)
        lines.append(jnp.sum(line, axis=0, keepdims=True))
    return lines


def forward(x, weights, saved, blocked):
    (wq, wk, wv), wproj, wup, wdown, gamma, beta = weights
    hat, scale = normalise(x)
    saved.hat1[...] = hat
    saved.scale1[...] = scale
    normed = hat.astype(BF16)
    saved.query[...] = dot(normed, wq).astype(BF16)
    saved.key[...] = dot(normed, wk).astype(BF16)
    saved.value[...] = dot(normed, wv).astype(BF16)
    bias = saved.bias[...]
    for w in range(WINDOWS):
        query = stack_heads(window(saved.query, w))
        score = dot(window(saved.key, w), query, (1, 1)) * (HEAD**-0.5) + bias
        if blocked is not None:
            score = jnp.where(blocked, -1e9, score)
        raised = jnp.exp(score - jnp.max(score, axis=0, keepdims=True))
        attn = raised / jnp.sum(raised, axis=0, keepdims=True)
        saved.attn[w] = attn
        mixed = merge_heads(dot(attn.astype(BF16), window(saved.value, w), (0, 0)))
        put_window(saved.mixed, w, mixed)
    hidden = x + dot(saved.mixed[...], wproj)
    hat, scale = normalise(hidden)
    saved.hat2[...] = hat
    saved.scale2[...] = scale
    up = dot(hat.astype(BF16), wup)
    square = up * up
    bent = jnp.tanh(GELU_A * up * (1.0 + GELU_B * square))
    half = 0.5 * (1.0 + bent)
    lifted = (up * half).astype(BF16)
    saved.lifted[...] = lifted
    saved.slope[...] = half + 0.5 * up * (1.0 - bent * bent) * (GELU_A * (1.0 + 3.0 * GELU_B * square))
    gdn = hidden + dot(lifted, wdown)
    power = beta + dot((gdn * gdn).astype(BF16), gamma)
    root = lax.rsqrt(power)
    saved.gdn[...] = gdn
    saved.root[...] = root
    return gdn * root


def backward(grad, weights, saved, pack):
    (wq, wk, wv), wproj, wup, wdown, gamma, beta = weights
    gdn = saved.gdn[...]
    root = saved.root[...]
    dpower = -0.5 * grad * gdn * (root * root * root)
    dpower_16 = dpower.astype(BF16)
    gamma_grad = dot((gdn * gdn).astype(BF16), dpower_16, (0, 0))
    for i in range(3):
        pack[C * i : C * (i + 1), C:128] = gamma_grad[:, 32 * i : 32 * (i + 1)].astype(BF16)
    beta_grad = jnp.sum(dpower, axis=0, keepdims=True)
    dgdn = grad * root + 2.0 * gdn * dot(dpower_16, gamma, (1, 1))
    dgdn_16 = dgdn.astype(BF16)
    down_grad = dot(dgdn_16, saved.lifted[...], (0, 0))
    for i in range(3):
        pack[672 + C * i : 672 + C * (i + 1), :] = down_grad[:, 128 * i : 128 * (i + 1)].astype(BF16)
    dup = (dot(dgdn_16, wdown, (1, 1)) * saved.slope[...]).astype(BF16)
    hat2 = saved.hat2[...]
    up_grad = dot(hat2.astype(BF16), dup, (0, 0))
    for i in range(3):
        pack[384 + C * i : 384 + C * (i + 1), :] = up_grad[:, 128 * i : 128 * (i + 1)].astype(BF16)
    dhidden = dgdn + norm_back(dot(dup, wup, (1, 1)), hat2, saved.scale2[...])
    dhidden_16 = dhidden.astype(BF16)
    proj_grad = dot(saved.mixed[...], dhidden_16, (0, 0))
    pack[288:384, 0:C] = proj_grad.astype(BF16)
    saved.dmixed[...] = dot(dhidden_16, wproj, (1, 1)).astype(BF16)
    total = jnp.zeros((TOKENS, HEADS * TOKENS), F32)
    for w in range(WINDOWS):
        dmixed = stack_heads(window(saved.dmixed, w))
        attn = saved.attn[w]
        dattn = dot(window(saved.value, w), dmixed, (1, 1))
        put_window(saved.dvalue, w, dot(attn.astype(BF16), dmixed))
        dscore = attn * (dattn - jnp.sum(attn * dattn, axis=0, keepdims=True))
        total = total + dscore
        dscore = (dscore * (HEAD**-0.5)).astype(BF16)
        put_window(saved.dkey, w, dot(dscore, stack_heads(window(saved.query, w))))
        put_window(saved.dquery, w, merge_heads(dot(dscore, window(saved.key, w), (0, 0))))
    lines = table_slots(total)
    hat1 = saved.hat1[...]
    normed = hat1.astype(BF16)
    dnormed = jnp.zeros((PIX, C), F32)
    for i, (part, weight) in enumerate(((saved.dquery, wq), (saved.dkey, wk), (saved.dvalue, wv))):
        piece = part[...]
        pack[C * i : C * (i + 1), 0:C] = dot(normed, piece, (0, 0)).astype(BF16)
        dnormed = dnormed + dot(piece, weight, (1, 1))
    edge = jnp.concatenate([beta_grad, jnp.zeros((1, 128 - C), F32)], axis=1)
    rows = [edge] + [line[:, 128 * i : 128 * (i + 1)] for line in lines for i in range(2)]
    rows.append(jnp.zeros((ROWS - 967, 128), F32))
    pack[960:ROWS, :] = jnp.concatenate(rows, axis=0).astype(BF16)
    return dhidden + norm_back(dnormed, hat1, saved.scale1[...])


class Saved:
    names = {
        "hat1": ((PIX, C), F32),
        "scale1": ((PIX, 1), F32),
        "query": ((PIX, C), BF16),
        "key": ((PIX, C), BF16),
        "value": ((PIX, C), BF16),
        "bias": ((TOKENS, HEADS * TOKENS), F32),
        "attn": ((WINDOWS, TOKENS, HEADS * TOKENS), F32),
        "mixed": ((PIX, C), BF16),
        "hat2": ((PIX, C), F32),
        "scale2": ((PIX, 1), F32),
        "lifted": ((PIX, HID), BF16),
        "slope": ((PIX, HID), F32),
        "gdn": ((PIX, C), F32),
        "root": ((PIX, C), F32),
        "dmixed": ((PIX, C), BF16),
        "dquery": ((PIX, C), BF16),
        "dkey": ((PIX, C), BF16),
        "dvalue": ((PIX, C), BF16),
    }

    def __init__(self, refs):
        for name, ref in zip(Saved.names, refs):
            setattr(self, name, ref)


def copy_to(src, dst, send, recv, device):
    return pltpu.make_async_remote_copy(
        src_ref=src, dst_ref=dst, send_sem=send, recv_sem=recv, device_id=device, device_id_type=MESH
    )


def read_weights(b, refs):
    wqkv, wproj, wup, wdown, gamma, beta = refs
    whole = wqkv[b].astype(F32)
    parts = tuple(whole[:, C * i : C * (i + 1)].astype(BF16) for i in range(3))
    return parts, wproj[b], wup[b], wdown[b], gamma[b].astype(BF16), beta[b : b + 1, :]


class Exchange:
    def __init__(self, b, n_lat, n_lon, pack, first, chunk, second, third, fourth, sems):
        self.b, self.n_lat, self.n_lon = b, n_lat, n_lon
        self.pack, self.first, self.chunk = pack, first, chunk
        self.second, self.third, self.fourth = second, third, fourth
        self.sems = sems
        self.rows = ROWS // n_lat
        self.tiles = self.rows // TILE
        self.owners = min(self.tiles, n_lon // 2)
        self.deep = self.rows // self.owners
        self.lat, self.lon = lax.axis_index("lat"), lax.axis_index("lon")

    def owner(self, t):
        return 2 * t + self.b

    def piece(self, ref, i):
        return ref.at[pl.ds(pl.multiple_of(i * self.rows, self.rows), self.rows), :]

    def lat_copy(self, o):
        to = lax.rem(self.lat + o, self.n_lat)
        send, recv = self.sems[0], self.sems[1]
        return copy_to(self.piece(self.pack, to), self.first.at[o], send.at[o], recv.at[o], (to, self.lon))

    def start_lat(self):
        def body(o, _):
            self.lat_copy(o).start()
            return 0

        lax.fori_loop(1, self.n_lat, body, 0)

    def add_lat(self):
        def body(o, _):
            self.lat_copy(o).wait()
            return 0

        lax.fori_loop(1, self.n_lat, body, 0)
        at = pl.ds(pl.multiple_of(self.lat * self.rows, self.rows), self.rows)
        total = self.pack[at, :].astype(F32)
        for o in range(1, self.n_lat):
            total = total + self.first[o].astype(F32)
        self.chunk[...] = total.reshape(self.owners, self.deep, 128)

    def lon_copy(self, t):
        send, recv = self.sems[2], self.sems[3]
        return copy_to(
            self.chunk.at[t], self.second.at[self.lon], send.at[t], recv.at[self.lon], (self.lat, self.owner(t))
        )

    def start_lon(self):
        def body(t, _):
            @pl.when(self.owner(t) != self.lon)
            def _():
                self.lon_copy(t).start()

            return 0

        lax.fori_loop(0, self.owners, body, 0)

    def gather_copy(self, o):
        send, recv = self.sems[4], self.sems[5]
        to = lax.rem(self.lon + o, self.n_lon)
        mine = self.lon // 2
        return copy_to(self.third.at[mine], self.third.at[mine], send.at[o], recv.at[mine], (self.lat, to))

    def add_lon(self, factor):
        def sent(t, _):
            @pl.when(self.owner(t) != self.lon)
            def _():
                self.lon_copy(t).wait_send()

            return 0

        lax.fori_loop(0, self.owners, sent, 0)

        @pl.when(lax.rem(self.lon, 2) == self.b)
        def _():
            mine = self.lon // 2

            def arrived(o, _):
                source = lax.rem(self.lon + o, self.n_lon)
                pltpu.make_async_copy(self.second.at[source], self.second.at[source], self.sems[3].at[source]).wait()
                return 0

            lax.fori_loop(1, self.n_lon, arrived, 0)
            self.second[self.lon] = self.chunk[mine]
            total = self.second[0]
            for i in range(1, self.n_lon):
                total = total + self.second[i]
            self.third[mine] = total * factor

            def give(o, _):
                self.gather_copy(o).start()
                return 0

            lax.fori_loop(1, self.n_lon, give, 0)

    def fourth_copy(self, o):
        to = lax.rem(self.lat + o, self.n_lat)
        send, recv = self.sems[6], self.sems[7]
        place = self.piece(self.fourth, self.lat)
        return copy_to(place, place, send.at[o], recv.at[self.lat], (to, self.lon))

    def finish_lon(self):
        @pl.when(lax.rem(self.lon, 2) == self.b)
        def _():
            def sent(o, _):
                self.gather_copy(o).wait_send()
                return 0

            lax.fori_loop(1, self.n_lon, sent, 0)

        def arrived(t, _):
            @pl.when(self.owner(t) != self.lon)
            def _():
                pltpu.make_async_copy(self.third.at[t], self.third.at[t], self.sems[5].at[t]).wait()

            return 0

        lax.fori_loop(0, self.owners, arrived, 0)
        at = pl.ds(pl.multiple_of(self.lat * self.rows, self.rows), self.rows)
        self.fourth[at, :] = self.third[...].reshape(self.rows, 128).astype(BF16)

        def give(o, _):
            self.fourth_copy(o).start()
            return 0

        lax.fori_loop(1, self.n_lat, give, 0)

    def finish_lat(self):
        def body(o, _):
            self.fourth_copy(o).wait_send()
            source = lax.rem(self.lat + o, self.n_lat)
            place = self.piece(self.fourth, source)
            pltpu.make_async_copy(place, place, self.sems[7].at[source]).wait()
            return 0

        lax.fori_loop(1, self.n_lat, body, 0)


def exchange_scratch(n_lat, n_lon):
    rows = ROWS // n_lat
    owners = min(rows // TILE, n_lon // 2)
    deep = rows // owners
    dma = pltpu.SemaphoreType.DMA
    return [
        pltpu.VMEM((ROWS, 128), BF16),
        pltpu.VMEM((n_lat, rows, 128), BF16),
        pltpu.VMEM((owners, deep, 128), F32),
        pltpu.VMEM((n_lon, deep, 128), F32),
        pltpu.VMEM((owners, deep, 128), F32),
        pltpu.VMEM((ROWS, 128), BF16),
        dma((n_lat,)),
        dma((n_lat,)),
        dma((owners,)),
        dma((n_lon,)),
        dma((n_lon,)),
        dma((owners,)),
        dma((n_lat,)),
        dma((n_lat,)),
    ]


def unpack(b, total, outs):
    qkv, proj, up, down, gamma, beta, table = outs
    first = total[0:288, :].astype(F32)
    parts = [first[C * i : C * (i + 1)] for i in range(3)]
    qkv[b] = jnp.concatenate([part[:, 0:C] for part in parts], axis=1)
    gamma[b] = jnp.concatenate([part[:, C:128] for part in parts], axis=1)
    proj[b] = total[288:384, 0:C].astype(F32)
    for i in range(3):
        up[b, :, 128 * i : 128 * (i + 1)] = total[384 + C * i : 384 + C * (i + 1), :].astype(F32)
        block = total[672 + C * i : 672 + C * (i + 1), :].astype(F32)
        down[b, 128 * i : 128 * (i + 1), :] = block.T
    edge = total[960:976, :].astype(F32)
    beta[b : b + 1, :] = edge[0:1, 0:C]
    lines = [jnp.concatenate([edge[1 + 2 * h : 2 + 2 * h], edge[2 + 2 * h : 3 + 2 * h]], axis=1) for h in range(HEADS)]
    table[b] = dot(jnp.concatenate(lines, axis=0).astype(BF16), rel_slots().astype(BF16), (1, 1))


def kernel(n_lat, n_lon, *refs):
    refs = list(refs)

    def take(count):
        taken = refs[:count]
        del refs[:count]
        return taken

    sig, cot = take(2)
    weight_refs = take(6)
    (table,) = take(1)
    decoded, sgrad = take(2)
    grad_outs = take(7)
    saved = [Saved(take(len(Saved.names))) for _ in range(2)]
    field, send_out, send_cot, send_dec, send_grad = take(5)
    south, east, corner, halo_send, halo_recv = take(5)
    exchanges = []
    for b in range(2):
        parts = take(14)
        exchanges.append(Exchange(b, n_lat, n_lon, *parts[:6], parts[6:]))
    lat, lon = lax.axis_index("lat"), lax.axis_index("lon")
    above, below = lax.rem(lat + n_lat - 1, n_lat), lax.rem(lat + 1, n_lat)
    west, easterly = lax.rem(lon + n_lon - 1, n_lon), lax.rem(lon + 1, n_lon)

    barrier = pltpu.get_barrier_semaphore()

    def greet(device):
        pl.semaphore_signal(barrier, inc=1, device_id=device, device_id_type=MESH)

    def greet_lat(o, _):
        greet((lax.rem(lat + o, n_lat), lon))
        return 0

    def greet_lon(o, _):
        greet((lat, lax.rem(lon + o, n_lon)))
        return 0

    lax.fori_loop(1, n_lat, greet_lat, 0)
    lax.fori_loop(1, n_lon, greet_lon, 0)
    greet((above, west))
    greet((below, easterly))

    def halo(i, whole, whole_rows, side, side_rows, both_rows, devices):
        copies = []
        rows = (whole_rows, side_rows, both_rows)
        targets = (south, east, corner)
        for j in range(3):
            src = whole.at[pl.ds(rows[j][0], rows[j][1]), :]
            k = 3 * i + j
            copies.append(copy_to(src, targets[j].at[i], halo_send.at[k], halo_recv.at[k], devices[j]))
        return copies

    def up_halo(i, ref):
        return halo(
            i, ref, (0, HALF), ref, (HALF, UNIT), (0, UNIT), ((above, lon), (lat, west), (above, west))
        )

    def down_halo(i, ref):
        return halo(
            i,
            ref,
            (HALF, HALF),
            ref,
            (HALF - UNIT, UNIT),
            (PIX - UNIT, UNIT),
            ((below, lon), (lat, easterly), (below, easterly)),
        )

    def shifted(i, ref):
        parts = [ref[HALF + UNIT : PIX, :], east[i], south[i, UNIT:HALF, :], corner[i]]
        return jnp.concatenate([part.astype(F32) for part in parts], axis=0)

    def unshifted(i, ref):
        parts = [corner[i], south[i, 0 : HALF - UNIT, :], east[i], ref[0 : HALF - UNIT, :]]
        return jnp.concatenate([part.astype(F32) for part in parts], axis=0)

    unfold(sig, field)
    unfold(cot, send_cot)
    for b in range(2):
        build_bias(table[b], saved[b].bias)
    weights = [read_weights(b, weight_refs) for b in range(2)]
    output = forward(field[...], weights[0], saved[0], None)
    send_out[...] = output.astype(BF16)

    pl.semaphore_wait(barrier, n_lat + n_lon)
    out_copies = up_halo(0, send_out)
    cot_copies = up_halo(1, send_cot)
    for copy in out_copies + cot_copies:
        copy.start()
    for copy in out_copies:
        copy.wait()
    is_last = (lat == n_lat - 1).astype(jnp.int32)
    shape = (TOKENS, HEADS * TOKENS)
    differ = (iota(shape, 0) // 32 != (iota(shape, 1) % TOKENS) // 32).astype(jnp.int32)
    blocked = differ * is_last > 0
    output = forward(shifted(0, send_out), weights[1], saved[1], blocked)
    send_dec[...] = output.astype(BF16)
    dec_copies = down_halo(2, send_dec)
    for copy in dec_copies:
        copy.start()
    for copy in cot_copies:
        copy.wait()
    back = backward(shifted(1, send_cot), weights[1], saved[1], exchanges[1].pack)
    send_grad[...] = back.astype(BF16)
    grad_copies = down_halo(3, send_grad)
    for copy in grad_copies:
        copy.start()
    exchanges[1].start_lat()
    for copy in dec_copies:
        copy.wait()
    fold(unshifted(2, send_dec), decoded)
    for copy in grad_copies:
        copy.wait()
    back = backward(unshifted(3, send_grad), weights[0], saved[0], exchanges[0].pack)
    fold(back, sgrad)
    exchanges[0].start_lat()
    factor = 1.0 / math.sqrt(PIX * n_lat * n_lon)
    for step in ("add_lat", "start_lon", "add_lon", "finish_lon", "finish_lat"):
        for b in (1, 0):
            method = getattr(exchanges[b], step)
            if step == "add_lon":
                method(factor)
            else:
                method()
    for b in (1, 0):
        unpack(b, exchanges[b].fourth, grad_outs)


def solution(mesh):
    n_lat, n_lon = mesh.shape["lat"], mesh.shape["lon"]

    def per_device(sig, cot, wqkv, wproj, wup, wdown, gamma, beta, table):
        dma = pltpu.SemaphoreType.DMA
        saved = [pltpu.VMEM(shape, kind) for shape, kind in Saved.names.values()]
        scratch = saved + saved
        scratch += [pltpu.VMEM((PIX, C), F32)] + [pltpu.VMEM((PIX, C), BF16)] * 4
        scratch += [
            pltpu.VMEM((4, HALF, C), BF16),
            pltpu.VMEM((4, UNIT, C), BF16),
            pltpu.VMEM((4, UNIT, C), BF16),
            dma((12,)),
            dma((12,)),
        ]
        for _ in range(2):
            scratch += exchange_scratch(n_lat, n_lon)
        shapes = [(sig.shape, BF16), (cot.shape, BF16)]
        shapes += [(leaf.shape, F32) for leaf in (wqkv, wproj, wup, wdown, gamma, beta, table)]
        vmem = pl.BlockSpec(memory_space=pltpu.VMEM)
        return pl.pallas_call(
            functools.partial(kernel, n_lat, n_lon),
            out_shape=[jax.ShapeDtypeStruct(shape, kind) for shape, kind in shapes],
            in_specs=[vmem] * 9,
            out_specs=[vmem] * 9,
            scratch_shapes=scratch,
            compiler_params=pltpu.CompilerParams(
                collective_id=0, has_side_effects=True, vmem_limit_bytes=48 * 1024 * 1024
            ),
        )(sig, cot, wqkv, wproj, wup, wdown, gamma, beta, table)

    in_specs = (P("lat", "lon"), P("lat", "lon"), P(), P(), P(), P(), P(), P(), P())
    out_specs = (P("lat", "lon"), P("lat", "lon"), P(), P(), P(), P(), P(), P(), P())
    return jax.shard_map(per_device, mesh=mesh, in_specs=in_specs, out_specs=out_specs, check_vma=False)
```

time: 472 us -> 71.5 us (0.15)
  waiting for transfers between devices: 261 us -> 0 us
  blocking collectives: 80 us -> 0 us
  Pallas kernels: 0 us -> 60 us
  local copies, waits for them, and re-layouts: 47 us -> 10.5 us
  matrix products: 32 us -> 0 us
  other arithmetic: 25.3 us -> 0 us
  between operations: 15.9 us -> 0.71 us
  starting transfers between devices: 9.59 us -> 0 us
    psum x1 -> x0, waiting for transfers between devices: 251 us -> none  [per_device(): lax.psum((jnp.stack([qkv_one, qkv_two]), jnp.stack([proj_one, proj_two]),...]
    psum x1 -> x0, blocking collectives: 80 us -> none  [per_device(): lax.psum((jnp.stack([qkv_one, qkv_two]), jnp.stack([proj_one, proj_two]),...]
    pallas_call x0 -> x1, Pallas kernels: none -> 60 us  [per_device(): pl.pallas_call(functools.partial(kernel, n_lat, n_lon), out_shape=[jax.Sh...]
    dot_general x44 -> x0, matrix products: 30 us -> none  [the longest x4 7.79 us: swin_block(): jnp.dot(rel_table, offset_table().T, precision=lax.Precision.HIGHEST)]
    convert_element_type x28 -> x0, local copies, waits for them, and re-layouts: 13.4 us -> none  [the longest x8 5.24 us: swin_block(): (mixed_out * lax.rsqrt(gdn_power)).reshape(rows_in, cols_in, C)]
    ppermute x6 -> x0, waiting for transfers between devices: 9.91 us -> none  [from_behind(): return lax.ppermute(block, axis, route)]
    ppermute x6 -> x0, starting transfers between devices: 9.55 us -> none  [from_behind(): return lax.ppermute(block, axis, route)]
    reshape x14 -> x0, local copies, waits for them, and re-layouts: 6.07 us -> none  [the longest x4 2.65 us: swin_block(): mixed_heads = mixed_heads.astype(jnp.bfloat16).reshape(-1, C)]
  transfers between devices with their start and end apart: 7 -> 0, of which waited for: 4 -> 0; matrix products, arithmetic and copies ran while one was open for 7% -> 0% of each run, Pallas kernels for 0% -> 0%
where the time goes in v1:
time: 71.5 us; the launch traced here: 71.3 us
  Pallas kernels  60 us (84%)
  local copies, waits for them, and re-layouts  10.5 us (15%)
    pallas_call x1, Pallas kernels, per_device(): pl.pallas_call(functools.partial(kernel, n_lat, n_lon), out_shape=[jax.Sh...  60 us
    unnamed x23, local copies, waits for them, and re-layouts  9.05 us
    pallas_call x2, local copies, waits for them, and re-layouts, per_device(): pl.pallas_call(functools.partial(kernel, n_lat, n_lon), out_shape=[jax.Sh...  1.47 us

profile of v1, /device:TPU:1, one launch (start us, length us, event | category | flops | bytes accessed | tf_op | source)
XLA Modules:
  0.0 71.3 jit_solution(8745134563537529019)
XLA Ops:
  0.6 0.0 copy-start.6
  0.7 0.7 copy.19.refs_8_
  1.4 0.0 copy-start
  1.4 0.0 copy-start.1
  1.4 0.0 copy-start.5
  1.4 1.1 %copy.18.refs_5_ = bf16[2,384,96]{2,1,0:T(8,128)(2,1)S(1)} copy(bf16[2,384,96]{1,2,0:T(8,128)(2,1)} %param.14) | data formatting | bytes 294912 | tf_op args[5]
  2.5 0.0 copy-done.6
  2.5 0.0 copy-done
  2.5 0.0 copy-done.1
  2.5 0.0 copy-done.5
  2.5 0.0 copy-start.2
  2.5 0.9 %copy-done.2 = bf16[8,6144]{1,0:T(8,128)(2,1)S(1)} copy-done((bf16[8,6144]{1,0:T(8,128)(2,1)S(1)}, bf16[8,6144]{1,0:T(8,128)(2,1)}, u32[]{:S(2)}) %copy-start.2) | copy-done | bytes 98328
  3.4 0.0 copy-start.3
  3.4 0.9 %copy-done.3 = bf16[8,6144]{1,0:T(8,128)(2,1)S(1)} copy-done((bf16[8,6144]{1,0:T(8,128)(2,1)S(1)}, bf16[8,6144]{1,0:T(8,128)(2,1)}, u32[]{:S(2)}) %copy-start.3) | copy-done | bytes 98328
  4.3 0.0 copy-start.4
  4.3 0.9 %copy-done.4 = f32[2,96,96]{2,1,0:T(8,128)S(1)} copy-done((f32[2,96,96]{2,1,0:T(8,128)S(1)}, f32[2,96,96]{2,1,0:T(8,128)}, u32[]{:S(2)}) %copy-start.4) | copy-done | bytes 73752
  5.2 60.0 %shard_map.160 = (bf16[8,6144]{1,0:T(8,128)(2,1)S(1)}, bf16[8,6144]{1,0:T(8,128)(2,1)S(1)}, f32[2,96,288]{2,1,0:T(8,128)S(1)}, f32[2,96,96]{2,1,0:T(8,128)S(1)},...) custom-call(bf16[8,6144]{1,0:T(8,128)(2,1)S(1)} %copy-done.2, ...), custom_call_target="tpu_custom_call" | custom-call | tf_op jit(solution)/shard_map/pallas_call | solution.py:625
  65.2 0.6 copy.21
  65.8 0.9 %copy.20 = f32[2,384,96]{1,2,0:T(8,128)} copy(f32[2,384,96]{2,1,0:T(8,128)S(1)} %get-tuple-element.14) | data formatting | bytes 589824 | tf_op jit(solution)/shard_map/pallas_call | solution.py:625
  66.7 0.6 copy.29
  67.4 0.6 copy.30
  68.0 0.7 %copy.31 = f32[2,96,288]{2,1,0:T(8,128)} copy(f32[2,96,288]{2,1,0:T(8,128)S(1)} %get-tuple-element.29) | data formatting | bytes 442368
  68.7 0.6 copy.32
  69.3 0.7 %copy.33 = f32[2,96,384]{2,1,0:T(8,128)} copy(f32[2,96,384]{2,1,0:T(8,128)S(1)} %get-tuple-element.31) | data formatting | bytes 589824
  70.1 0.6 copy.34
  70.7 0.6 copy.35
Async XLA Ops:
  0.6 1.8 %copy-start.6 = (f32[2,96]{1,0:T(2,128)S(1)}, f32[2,96]{1,0:T(2,128)}, u32[]{:S(2)}) copy-start(f32[2,96]{1,0:T(2,128)} %refs_7_.1) | copy-start | bytes 2308
  1.4 1.1 %copy-start = (bf16[2,96,288]{2,1,0:T(8,128)(2,1)S(1)}, bf16[2,96,288]{2,1,0:T(8,128)(2,1)}, u32[]{:S(2)}) copy-start(bf16[2,96,288]{2,1,0:T(8,128)(2,1)} %refs_2_.1) | copy-start | bytes 331780
  1.4 1.2 %copy-start.1 = (bf16[2,96,384]{2,1,0:T(8,128)(2,1)S(1)}, bf16[2,96,384]{2,1,0:T(8,128)(2,1)}, u32[]{:S(2)}) copy-start(bf16[2,96,384]{2,1,0:T(8,128)(2,1)} %refs_4_.1) | copy-start | bytes 442372
  1.4 1.2 %copy-start.5 = (bf16[2,96,96]{2,1,0:T(8,128)(2,1)S(1)}, bf16[2,96,96]{2,1,0:T(8,128)(2,1)}, u32[]{:S(2)}) copy-start(bf16[2,96,96]{2,1,0:T(8,128)(2,1)} %refs_3_.1) | copy-start | bytes 110596
  2.5 0.9 %copy-start.2 = (bf16[8,6144]{1,0:T(8,128)(2,1)S(1)}, bf16[8,6144]{1,0:T(8,128)(2,1)}, u32[]{:S(2)}) copy-start(bf16[8,6144]{1,0:T(8,128)(2,1)} %refs_0_.1) | copy-start | bytes 294916
  3.4 0.9 %copy-start.3 = (bf16[8,6144]{1,0:T(8,128)(2,1)S(1)}, bf16[8,6144]{1,0:T(8,128)(2,1)}, u32[]{:S(2)}) copy-start(bf16[8,6144]{1,0:T(8,128)(2,1)} %refs_1_.1) | copy-start | bytes 294916
  4.3 0.9 %copy-start.4 = (f32[2,96,96]{2,1,0:T(8,128)S(1)}, f32[2,96,96]{2,1,0:T(8,128)}, u32[]{:S(2)}) copy-start(f32[2,96,96]{2,1,0:T(8,128)} %refs_6_.1) | copy-start | bytes 221188

commit v2 on v1

v2 whole, which is shorter than its diff:
```python
import functools
import math

import jax
import jax.numpy as jnp
from jax import lax
from jax.experimental import pallas as pl
from jax.experimental.pallas import tpu as pltpu
from jax.sharding import PartitionSpec as P

C = 96
HEADS = 3
HEAD = 32
HID = 384
WIN = 8
RELS = 225
SLOTS = 256
PIX = 512
HALF = 256
UNIT = 16
WINDOWS = 8
TOKENS = 64
ROWS = 1024
QUAD = 4
EPS = 1e-05
GELU_A = math.sqrt(2.0 / math.pi)
GELU_B = 0.044715
MESH = pl.DeviceIdType.MESH
F32 = jnp.float32
BF16 = jnp.bfloat16


def iota(shape, dim):
    return lax.broadcasted_iota(jnp.int32, shape, dim)


def dot(a, b, over=(1, 0)):
    return lax.dot_general(a, b, (((over[0],), (over[1],)), ((), ())), preferred_element_type=F32)


def dot_split(a, b):
    high = a.astype(BF16)
    rest = a - high.astype(F32)
    middle = rest.astype(BF16)
    low = (rest - middle.astype(F32)).astype(BF16)
    return dot(high, b) + dot(middle, b) + dot(low, b)


def row_mean(a):
    return jnp.sum(a, axis=-1, keepdims=True) * (1.0 / C)


def normalise(v):
    center = v - row_mean(v)
    scale = lax.rsqrt(row_mean(center * center) + EPS)
    return center * scale, scale


def norm_back(grad, hat, scale):
    return scale * (grad - row_mean(grad) - hat * row_mean(grad * hat))


def stack_heads(a):
    head_of = iota(a.shape, 1) // HEAD
    zero = jnp.zeros_like(a)
    return jnp.concatenate([jnp.where(head_of == h, a, zero) for h in range(HEADS)], axis=0)


def merge_heads(a):
    parts = [a[h * TOKENS : (h + 1) * TOKENS] for h in range(HEADS)]
    head_of = iota((TOKENS, C), 1) // HEAD
    return jnp.where(head_of == 0, parts[0], jnp.where(head_of == 1, parts[1], parts[2]))


def window(ref, w):
    step = TOKENS // 2
    upper = ref[w * step : (w + 1) * step, :]
    lower = ref[HALF + w * step : HALF + (w + 1) * step, :]
    return jnp.concatenate([upper, lower], axis=0)


def put_window(ref, w, value):
    step = TOKENS // 2
    ref[w * step : (w + 1) * step, :] = value[:step].astype(ref.dtype)
    ref[HALF + w * step : HALF + (w + 1) * step, :] = value[step:].astype(ref.dtype)


def unfold(src, dst):
    low = iota((WIN, C), 0) < 4
    for group in range(16):
        part = src[:, group * 4 * C : (group + 1) * 4 * C].astype(F32)
        for pair in range(2):
            one = part[:, (2 * pair) * C : (2 * pair + 1) * C]
            two = part[:, (2 * pair + 1) * C : (2 * pair + 2) * C]
            at = (group * 2 + pair) * 8
            dst[at : at + 8, :] = jnp.where(low, one, pltpu.roll(two, 4, 0)).astype(dst.dtype)
            dst[HALF + at : HALF + at + 8, :] = jnp.where(low, pltpu.roll(one, 4, 0), two).astype(dst.dtype)


def fold(value, dst):
    low = iota((WIN, C), 0) < 4
    for group in range(16):
        parts = []
        for pair in range(2):
            at = (group * 2 + pair) * 8
            upper = value[at : at + 8]
            lower = value[HALF + at : HALF + at + 8]
            parts.append(jnp.where(low, upper, pltpu.roll(lower, 4, 0)))
            parts.append(jnp.where(low, pltpu.roll(upper, 4, 0), lower))
        dst[:, group * 4 * C : (group + 1) * 4 * C] = jnp.concatenate(parts, axis=1).astype(dst.dtype)


def rel_slots():
    entry = iota((RELS, SLOTS), 0)
    slot = iota((RELS, SLOTS), 1)
    return ((entry // 15 == slot % 16) & (entry % 15 == slot // 16)).astype(F32)


def spread_queries():
    query = iota((HEADS * TOKENS, HEADS * 128), 0)
    place = iota((HEADS * TOKENS, HEADS * 128), 1)
    inside = query % TOKENS
    row = (inside // 32) * 4 + inside % 4
    column = (inside % 32) // 4
    return ((query // TOKENS) * 128 + column * 16 + row == place).astype(F32)


def build_bias(table, bias):
    slots = dot_split(table, rel_slots().astype(BF16))
    sub = iota((8, SLOTS), 0)
    heads = []
    for h in range(HEADS):
        line = jnp.broadcast_to(slots[h : h + 1], (8, SLOTS))
        skew = line
        for s in range(1, 8):
            skew = jnp.where(sub == s, pltpu.roll(line, 16 * (s // 4) + s % 4, 1), skew)
        groups = []
        for g in range(8):
            turn = SLOTS - 119 + 32 * (g % 4) + 4 * (g // 4)
            groups.append(pltpu.roll(skew, turn % SLOTS, 1)[:, :128])
        heads.append(jnp.concatenate(groups, axis=0))
    wide = jnp.concatenate(heads, axis=1)
    back = spread_queries().astype(BF16)
    high = wide.astype(BF16)
    rest = wide - high.astype(F32)
    middle = rest.astype(BF16)
    low = (rest - middle.astype(F32)).astype(BF16)
    bias[...] = dot(high, back, (1, 1)) + dot(middle, back, (1, 1)) + dot(low, back, (1, 1))


def table_slots(total):
    wide = dot(total.astype(BF16), spread_queries().astype(BF16))
    sub = iota((8, SLOTS), 0)
    blank = jnp.zeros((8, 128), F32)
    lines = []
    for h in range(HEADS):
        skew = jnp.zeros((8, SLOTS), F32)
        for g in range(8):
            part = jnp.concatenate([wide[8 * g : 8 * g + 8, 128 * h : 128 * h + 128], blank], axis=1)
            skew = skew + pltpu.roll(part, 119 - 32 * (g % 4) - 4 * (g // 4), 1)
        line = skew
        for s in range(1, 8):
            line = jnp.where(sub == s, pltpu.roll(skew, SLOTS - 16 * (s // 4) - s % 4, 1), line)
        lines.append(jnp.sum(line, axis=0, keepdims=True))
    return lines


def forward(x, weights, saved, blocked):
    (wq, wk, wv), wproj, wup, wdown, gamma, beta = weights
    hat, scale = normalise(x)
    saved.hat1[...] = hat
    saved.scale1[...] = scale
    normed = hat.astype(BF16)
    saved.query[...] = dot(normed, wq).astype(BF16)
    saved.key[...] = dot(normed, wk).astype(BF16)
    saved.value[...] = dot(normed, wv).astype(BF16)
    bias = saved.bias[...]
    for w in range(WINDOWS):
        query = stack_heads(window(saved.query, w))
        score = dot(window(saved.key, w), query, (1, 1)) * (HEAD**-0.5) + bias
        if blocked is not None:
            score = jnp.where(blocked, -1e9, score)
        raised = jnp.exp(score - jnp.max(score, axis=0, keepdims=True))
        attn = raised / jnp.sum(raised, axis=0, keepdims=True)
        saved.attn[w] = attn
        mixed = merge_heads(dot(attn.astype(BF16), window(saved.value, w), (0, 0)))
        put_window(saved.mixed, w, mixed)
    hidden = x + dot(saved.mixed[...], wproj)
    hat, scale = normalise(hidden)
    saved.hat2[...] = hat
    saved.scale2[...] = scale
    up = dot(hat.astype(BF16), wup)
    square = up * up
    bent = jnp.tanh(GELU_A * up * (1.0 + GELU_B * square))
    half = 0.5 * (1.0 + bent)
    lifted = (up * half).astype(BF16)
    saved.lifted[...] = lifted
    saved.slope[...] = half + 0.5 * up * (1.0 - bent * bent) * (GELU_A * (1.0 + 3.0 * GELU_B * square))
    gdn = hidden + dot(lifted, wdown, (1, 1))
    power = beta + dot((gdn * gdn).astype(BF16), gamma)
    root = lax.rsqrt(power)
    saved.gdn[...] = gdn
    saved.root[...] = root
    return gdn * root


def backward(grad, weights, saved, pack, early=None):
    (wq, wk, wv), wproj, wup, wdown, gamma, beta = weights
    gdn = saved.gdn[...]
    root = saved.root[...]
    dpower = -0.5 * grad * gdn * (root * root * root)
    dpower_16 = dpower.astype(BF16)
    gamma_grad = dot((gdn * gdn).astype(BF16), dpower_16, (0, 0))
    for i in range(3):
        pack[576 + C * i : 576 + C * (i + 1), C:128] = gamma_grad[:, 32 * i : 32 * (i + 1)].astype(BF16)
    beta_grad = jnp.sum(dpower, axis=0, keepdims=True)
    dgdn = grad * root + 2.0 * gdn * dot(dpower_16, gamma, (1, 1))
    dgdn_16 = dgdn.astype(BF16)
    down_grad = dot(dgdn_16, saved.lifted[...], (0, 0))
    for i in range(3):
        pack[288 + C * i : 288 + C * (i + 1), :] = down_grad[:, 128 * i : 128 * (i + 1)].astype(BF16)
    dup = (dot(dgdn_16, wdown) * saved.slope[...]).astype(BF16)
    hat2 = saved.hat2[...]
    up_grad = dot(hat2.astype(BF16), dup, (0, 0))
    for i in range(3):
        pack[C * i : C * (i + 1), :] = up_grad[:, 128 * i : 128 * (i + 1)].astype(BF16)
    dhidden = dgdn + norm_back(dot(dup, wup, (1, 1)), hat2, saved.scale2[...])
    dhidden_16 = dhidden.astype(BF16)
    proj_grad = dot(saved.mixed[...], dhidden_16, (0, 0))
    pack[864:960, 0:C] = proj_grad.astype(BF16)
    saved.dmixed[...] = dot(dhidden_16, wproj, (1, 1)).astype(BF16)
    if early is not None:
        early()
    total = jnp.zeros((TOKENS, HEADS * TOKENS), F32)
    for w in range(WINDOWS):
        dmixed = stack_heads(window(saved.dmixed, w))
        attn = saved.attn[w]
        dattn = dot(window(saved.value, w), dmixed, (1, 1))
        put_window(saved.dvalue, w, dot(attn.astype(BF16), dmixed))
        dscore = attn * (dattn - jnp.sum(attn * dattn, axis=0, keepdims=True))
        total = total + dscore
        dscore = (dscore * (HEAD**-0.5)).astype(BF16)
        put_window(saved.dkey, w, dot(dscore, stack_heads(window(saved.query, w))))
        put_window(saved.dquery, w, merge_heads(dot(dscore, window(saved.key, w), (0, 0))))
    lines = table_slots(total)
    hat1 = saved.hat1[...]
    normed = hat1.astype(BF16)
    dnormed = jnp.zeros((PIX, C), F32)
    for i, (part, weight) in enumerate(((saved.dquery, wq), (saved.dkey, wk), (saved.dvalue, wv))):
        piece = part[...]
        pack[576 + C * i : 576 + C * (i + 1), 0:C] = dot(normed, piece, (0, 0)).astype(BF16)
        dnormed = dnormed + dot(piece, weight, (1, 1))
    edge = jnp.concatenate([beta_grad, jnp.zeros((1, 128 - C), F32)], axis=1)
    rows = [edge] + [line[:, 128 * i : 128 * (i + 1)] for line in lines for i in range(2)]
    rows.append(jnp.zeros((ROWS - 967, 128), F32))
    pack[960:ROWS, :] = jnp.concatenate(rows, axis=0).astype(BF16)
    return dhidden + norm_back(dnormed, hat1, saved.scale1[...])


class Saved:
    names = {
        "hat1": ((PIX, C), F32),
        "scale1": ((PIX, 1), F32),
        "query": ((PIX, C), BF16),
        "key": ((PIX, C), BF16),
        "value": ((PIX, C), BF16),
        "bias": ((TOKENS, HEADS * TOKENS), F32),
        "attn": ((WINDOWS, TOKENS, HEADS * TOKENS), F32),
        "mixed": ((PIX, C), BF16),
        "hat2": ((PIX, C), F32),
        "scale2": ((PIX, 1), F32),
        "lifted": ((PIX, HID), BF16),
        "slope": ((PIX, HID), F32),
        "gdn": ((PIX, C), F32),
        "root": ((PIX, C), F32),
        "dmixed": ((PIX, C), BF16),
        "dquery": ((PIX, C), BF16),
        "dkey": ((PIX, C), BF16),
        "dvalue": ((PIX, C), BF16),
    }

    def __init__(self, refs):
        for name, ref in zip(Saved.names, refs):
            setattr(self, name, ref)


def copy_to(src, dst, send, recv, device):
    return pltpu.make_async_remote_copy(
        src_ref=src, dst_ref=dst, send_sem=send, recv_sem=recv, device_id=device, device_id_type=MESH
    )


def read_weights(b, refs):
    wqkv, wproj, wup, wdown, gamma, beta = refs
    whole = wqkv[b].astype(F32)
    parts = tuple(whole[:, C * i : C * (i + 1)].astype(BF16) for i in range(3))
    return parts, wproj[b], wup[b], wdown[b], gamma[b].astype(BF16), beta[b : b + 1, :]


class Exchange:
    def __init__(self, n_lat, n_lon, base, pack, total, first, planes, sems):
        self.n_lat, self.planes_n, self.size = n_lat, n_lon // QUAD, n_lat * QUAD
        self.base, self.pack, self.total = base, pack, total
        self.first, self.planes, self.sems = first, planes, sems
        self.rows = first.shape[1]
        self.lat, lon = lax.axis_index("lat"), lax.axis_index("lon")
        self.quad, self.z = lax.rem(lon, QUAD), lon // QUAD
        self.place = self.lat * QUAD + self.quad

    def piece(self, ref, i):
        return ref.at[pl.ds(pl.multiple_of(self.base + i * self.rows, UNIT), self.rows), :]

    def in_plane(self, make):
        def body(i, _):
            step = lax.rem(4 * i + 1, 7) + 1 if self.n_lat == 8 else i + 1
            for turn in (2, 1, 3, 0):
                make(step, turn).start()
            return 0

        lax.fori_loop(0, self.n_lat - 1, body, 0)
        for turn in (2, 1, 3):
            make(0, turn).start()

    def target(self, step, turn):
        lat = lax.rem(self.lat + step, self.n_lat)
        quad = lax.rem(self.quad + turn, QUAD)
        return lat * QUAD + quad, (lat, self.z * QUAD + quad)

    def scatter_copy(self, step, turn):
        place, device = self.target(step, turn)
        slot = self.first.at[step * QUAD + turn]
        return copy_to(self.piece(self.pack, place), slot, self.sems.at[0], self.sems.at[1], device)

    def gather_copy(self, step, turn):
        _, device = self.target(step, turn)
        mine = self.piece(self.total, self.place)
        return copy_to(mine, mine, self.sems.at[4], self.sems.at[5], device)

    def plane_copy(self, step):
        z = lax.rem(self.z + step, self.planes_n)
        slot = self.planes.at[self.z]
        device = (self.lat, z * QUAD + self.quad)
        return copy_to(slot, slot, self.sems.at[2], self.sems.at[3], device)

    def wait_both(self, ref, sem):
        for i in range(2):
            pltpu.make_async_copy(ref, ref, self.sems.at[sem + i]).wait()

    def start(self):
        self.in_plane(self.scatter_copy)

    def add_plane(self):
        self.wait_both(self.first.at[pl.ds(1, self.size - 1)], 0)
        total = self.piece(self.pack, self.place)[...].astype(F32)
        for i in range(1, self.size):
            total = total + self.first[i].astype(F32)
        self.planes[self.z] = total.astype(BF16)

        def body(step, _):
            self.plane_copy(step).start()
            return 0

        lax.fori_loop(1, self.planes_n, body, 0)

    def add_all(self, factor):
        if self.planes_n > 1:
            self.wait_both(self.planes.at[pl.ds(0, self.planes_n - 1)], 2)
        total = self.planes[0].astype(F32)
        for i in range(1, self.planes_n):
            total = total + self.planes[i].astype(F32)
        self.piece(self.total, self.place)[...] = (total * factor).astype(BF16)
        self.in_plane(self.gather_copy)

    def finish(self):
        self.wait_both(self.total.at[pl.ds(self.base, (self.size - 1) * self.rows), :], 4)


def exchange_scratch(n_lat, n_lon, rows):
    rows = rows // (n_lat * QUAD)
    return [
        pltpu.VMEM((n_lat * QUAD, rows, 128), BF16),
        pltpu.VMEM((n_lon // QUAD, rows, 128), BF16),
        pltpu.SemaphoreType.DMA((6,)),
    ]


def unpack(b, total, outs):
    qkv, proj, up, down, gamma, beta, table = outs
    first = total[576:864, :].astype(F32)
    parts = [first[C * i : C * (i + 1)] for i in range(3)]
    qkv[b] = jnp.concatenate([part[:, 0:C] for part in parts], axis=1)
    gamma[b] = jnp.concatenate([part[:, C:128] for part in parts], axis=1)
    proj[b] = total[864:960, 0:C].astype(F32)
    for i in range(3):
        up[b, :, 128 * i : 128 * (i + 1)] = total[C * i : C * (i + 1), :].astype(F32)
        down[b, :, 128 * i : 128 * (i + 1)] = total[288 + C * i : 288 + C * (i + 1), :].astype(F32)
    edge = total[960:976, :].astype(F32)
    beta[b : b + 1, :] = edge[0:1, 0:C]
    lines = [jnp.concatenate([edge[1 + 2 * h : 2 + 2 * h], edge[2 + 2 * h : 3 + 2 * h]], axis=1) for h in range(HEADS)]
    slots = jnp.concatenate(lines, axis=0).astype(BF16)
    table[:, b, :] = dot(slots, rel_slots().astype(BF16), (1, 1))


def unpack_kernel(dec, sgrad, total0, total1, *refs):
    outs, staged, totals, sems = refs[:9], refs[9:16], refs[16:18], refs[18]
    loads = [pltpu.make_async_copy(src, dst, sems.at[9 + i]) for i, (src, dst) in enumerate(zip((total0, total1), totals))]
    copies = [pltpu.make_async_copy(src, dst, sems.at[i]) for i, (src, dst) in enumerate(zip((dec, sgrad) + staged, outs))]
    for copy in loads + copies[:2]:
        copy.start()
    for b in range(2):
        loads[b].wait()
        unpack(b, totals[b], staged)
    for copy in copies[2:]:
        copy.start()
    for copy in copies:
        copy.wait()


def kernel(n_lat, n_lon, *refs):
    refs = list(refs)

    def take(count):
        taken = refs[:count]
        del refs[:count]
        return taken

    hbm_args = take(9)
    results = take(4)
    args = take(9)
    (arg_sems,) = take(1)
    saved = [Saved(take(len(Saved.names))) for _ in range(2)]
    field, send_out, send_cot, send_dec, send_grad = take(5)
    south, east, corner, halo_send, halo_recv = take(5)
    packs, fields, totals = take(2), take(2), take(2)
    (result_sems,) = take(1)
    whole = Exchange(n_lat, n_lon, 0, packs[1], totals[1], *take(3))
    upper = Exchange(n_lat, n_lon, 0, packs[0], totals[0], *take(3))
    lower = Exchange(n_lat, n_lon, ROWS // 2, packs[0], totals[0], *take(3))
    lat, lon = lax.axis_index("lat"), lax.axis_index("lon")
    above, below = lax.rem(lat + n_lat - 1, n_lat), lax.rem(lat + 1, n_lat)
    west, easterly = lax.rem(lon + n_lon - 1, n_lon), lax.rem(lon + 1, n_lon)

    stores = [
        pltpu.make_async_copy(src, dst, result_sems.at[i]) for i, (src, dst) in enumerate(zip(fields + totals, results))
    ]
    loads = [pltpu.make_async_copy(src, dst, arg_sems.at[i]) for i, (src, dst) in enumerate(zip(hbm_args, args))]
    for load in loads:
        load.start()
    barrier = pltpu.get_barrier_semaphore()

    def greet(device):
        pl.semaphore_signal(barrier, inc=1, device_id=device, device_id_type=MESH)

    def greet_plane(i, _):
        _, device = whole.target(i // QUAD, lax.rem(i, QUAD))
        greet(device)
        return 0

    def greet_planes(i, _):
        greet((lat, lax.rem(lon + QUAD * i, n_lon)))
        return 0

    planes_n = n_lon // QUAD
    lax.fori_loop(1, n_lat * QUAD, greet_plane, 0)
    lax.fori_loop(1, planes_n, greet_planes, 0)
    for device in ((lat, west), (lat, easterly), (above, west), (below, easterly)):
        greet(device)
    greetings = n_lat * QUAD + planes_n + 2

    def halo(i, ref, rows, devices):
        copies = []
        for j, target in enumerate((south, east, corner)):
            src = ref.at[pl.ds(rows[j][0], rows[j][1]), :]
            k = 3 * i + j
            copies.append(copy_to(src, target.at[i], halo_send.at[k], halo_recv.at[k], devices[j]))
        return copies

    def up_halo(i, ref):
        rows = ((0, HALF), (HALF, UNIT), (0, UNIT))
        return halo(i, ref, rows, ((above, lon), (lat, west), (above, west)))

    def down_halo(i, ref):
        rows = ((HALF, HALF), (HALF - UNIT, UNIT), (PIX - UNIT, UNIT))
        return halo(i, ref, rows, ((below, lon), (lat, easterly), (below, easterly)))

    def shifted(i, ref):
        parts = [ref[HALF + UNIT : PIX, :], east[i], south[i, UNIT:HALF, :], corner[i]]
        return jnp.concatenate([part.astype(F32) for part in parts], axis=0)

    def unshifted(i, ref):
        parts = [corner[i], south[i, 0 : HALF - UNIT, :], east[i], ref[0 : HALF - UNIT, :]]
        return jnp.concatenate([part.astype(F32) for part in parts], axis=0)

    for load in loads:
        load.wait()
    sig, cot, table = args[0], args[1], args[8]
    unfold(sig, field)
    unfold(cot, send_cot)
    for b in range(2):
        build_bias(table[:, b, :], saved[b].bias)
    weights = [read_weights(b, args[2:8]) for b in range(2)]
    output = forward(field[...], weights[0], saved[0], None)
    send_out[...] = output.astype(BF16)

    pl.semaphore_wait(barrier, greetings)
    out_copies = up_halo(0, send_out)
    cot_copies = up_halo(1, send_cot)
    for copy in out_copies + cot_copies:
        copy.start()
    for copy in out_copies:
        copy.wait()
    is_last = (lat == n_lat - 1).astype(jnp.int32)
    shape = (TOKENS, HEADS * TOKENS)
    differ = (iota(shape, 0) // 32 != (iota(shape, 1) % TOKENS) // 32).astype(jnp.int32)
    blocked = differ * is_last > 0
    output = forward(shifted(0, send_out), weights[1], saved[1], blocked)
    send_dec[...] = output.astype(BF16)
    dec_copies = down_halo(2, send_dec)
    for copy in dec_copies:
        copy.start()
    for copy in cot_copies:
        copy.wait()
    back = backward(shifted(1, send_cot), weights[1], saved[1], packs[1])
    send_grad[...] = back.astype(BF16)
    grad_copies = down_halo(3, send_grad)
    for copy in grad_copies:
        copy.start()
    whole.start()
    for copy in dec_copies:
        copy.wait()
    fold(unshifted(2, send_dec), fields[0])
    stores[0].start()
    for copy in grad_copies:
        copy.wait()
    factor = 1.0 / math.sqrt(PIX * n_lat * n_lon)

    def early():
        upper.start()
        whole.add_plane()

    back = backward(unshifted(3, send_grad), weights[0], saved[0], packs[0], early)
    lower.start()
    fold(back, fields[1])
    stores[1].start()
    whole.add_all(factor)
    upper.add_plane()
    lower.add_plane()
    upper.add_all(factor)
    lower.add_all(factor)
    whole.finish()
    stores[3].start()
    upper.finish()
    lower.finish()
    stores[2].start()
    for store in stores:
        store.wait()


def solution(mesh):
    n_lat, n_lon = mesh.shape["lat"], mesh.shape["lon"]

    def per_device(sig, cot, wqkv, wproj, wup, wdown, gamma, beta, table):
        dma = pltpu.SemaphoreType.DMA
        args = (sig, cot, wqkv, wproj, wup, jnp.swapaxes(wdown, 1, 2), gamma, beta, jnp.swapaxes(table, 0, 1))
        saved = [pltpu.VMEM(shape, kind) for shape, kind in Saved.names.values()]
        scratch = [pltpu.VMEM(arg.shape, arg.dtype) for arg in args] + [dma((9,))]
        scratch += saved + saved
        scratch += [pltpu.VMEM((PIX, C), F32)] + [pltpu.VMEM((PIX, C), BF16)] * 4
        scratch += [
            pltpu.VMEM((4, HALF, C), BF16),
            pltpu.VMEM((4, UNIT, C), BF16),
            pltpu.VMEM((4, UNIT, C), BF16),
            dma((12,)),
            dma((12,)),
        ]
        scratch += [pltpu.VMEM((ROWS, 128), BF16)] * 2 + [pltpu.VMEM(sig.shape, BF16)] * 2
        scratch += [pltpu.VMEM((ROWS, 128), BF16)] * 2 + [dma((4,))]
        scratch += exchange_scratch(n_lat, n_lon, ROWS)
        scratch += exchange_scratch(n_lat, n_lon, ROWS // 2) * 2
        hbm = pl.BlockSpec(memory_space=pltpu.HBM)
        field = jax.ShapeDtypeStruct(sig.shape, BF16)
        total = jax.ShapeDtypeStruct((ROWS, 128), BF16)
        results = pl.pallas_call(
            functools.partial(kernel, n_lat, n_lon),
            out_shape=[field, field, total, total],
            in_specs=[hbm] * 9,
            out_specs=[hbm] * 4,
            scratch_shapes=scratch,
            compiler_params=pltpu.CompilerParams(
                collective_id=0, has_side_effects=True, vmem_limit_bytes=62 * 1024 * 1024
            ),
        )(*args)
        grads = [jax.ShapeDtypeStruct(leaf.shape, F32) for leaf in args[2:]]
        outs = pl.pallas_call(
            unpack_kernel,
            out_shape=[field, field] + grads,
            in_specs=[hbm] * 4,
            out_specs=[hbm] * 9,
            scratch_shapes=[pltpu.VMEM(leaf.shape, F32) for leaf in args[2:]]
            + [pltpu.VMEM((ROWS, 128), BF16)] * 2
            + [dma((11,))],
            compiler_params=pltpu.CompilerParams(vmem_limit_bytes=62 * 1024 * 1024),
        )(*results)
        decoded, sgrad, qkv, proj, up, down, gammas, betas, tables = outs
        return decoded, sgrad, qkv, proj, up, jnp.swapaxes(down, 1, 2), gammas, betas, jnp.swapaxes(tables, 0, 1)

    in_specs = (P("lat", "lon"), P("lat", "lon"), P(), P(), P(), P(), P(), P(), P())
    out_specs = (P("lat", "lon"), P("lat", "lon"), P(), P(), P(), P(), P(), P(), P())
    return jax.shard_map(per_device, mesh=mesh, in_specs=in_specs, out_specs=out_specs, check_vma=False)
```

time: 71.5 us -> 58.9 us (0.82)
  local copies, waits for them, and re-layouts: 10.5 us -> 0 us
  Pallas kernels: 60 us -> 58.1 us
    unnamed x23 -> x0, local copies, waits for them, and re-layouts: 9.05 us -> none
    pallas_call x1 -> x2, Pallas kernels: 60 us -> 58.1 us  [the longest x1 51 us: per_device(): pl.pallas_call(functools.partial(kernel, n_lat, n_lon), out_shape=[field,...]
    pallas_call x2 -> x0, local copies, waits for them, and re-layouts: 1.47 us -> none  [per_device(): pl.pallas_call(functools.partial(kernel, n_lat, n_lon), out_shape=[jax.Sh...]
where the time goes in v2:
time: 58.9 us; the launch traced here: 58.8 us
  Pallas kernels  58.1 us (99%)
  between operations  0.65 us (1%)
    pallas_call x1, Pallas kernels, per_device(): pl.pallas_call(functools.partial(kernel, n_lat, n_lon), out_shape=[field,...  51 us
    pallas_call x1, Pallas kernels, per_device(): pl.pallas_call(unpack_kernel, out_shape=[field, field] + grads, in_specs=...  7.17 us

profile of v2, /device:TPU:1, one launch (start us, length us, event | category | flops | bytes accessed | tf_op | source)
XLA Modules:
  0.0 58.8 jit_solution(9851691288201476938)
XLA Ops:
  0.6 51.0 %shard_map.160 = (bf16[8,6144]{1,0:T(8,128)(2,1)}, bf16[8,6144]{1,0:T(8,128)(2,1)}, bf16[1024,128]{1,0:T(8,128)(2,1)}, bf16[1024,128]{1,0:T(8,128)(2,1)}) custom-call(bf16[8,6144]{1,0:T(8,128)(2,1)} %refs_0_.1, bf16[8,6144]{1,0:T(8,128)(2,1)} %refs_1_.1, bf16[2,96,288]{2,1,0:T(8,128)(2,1)} %refs_2_.1, bf16[2,96,96]{2,1,0:T(8,128)(2,1)} %refs_3_.1, ...), custom_call_target="tpu_custom_call" | custom-call | tf_op jit(solution)/shard_map/pallas_call | solution.py:583
  51.6 7.2 %shard_map.161 = (bf16[8,6144]{1,0:T(8,128)(2,1)}, bf16[8,6144]{1,0:T(8,128)(2,1)}, f32[2,96,288]{2,1,0:T(8,128)}, f32[2,96,96]{2,1,0:T(8,128)}, f32[2,96,384]{2...) custom-call(bf16[8,6144]{1,0:T(8,128)(2,1)} %get-tuple-element.22.dec, ...), custom_call_target="tpu_custom_call" | custom-call | tf_op jit(solution)/shard_map/pallas_call | solution.py:594

commit v3 on v2

--- a/solution.py
+++ b/solution.py
@@ -401,16 +401,19 @@
     table[:, b, :] = dot(slots, rel_slots().astype(BF16), (1, 1))
 
 
-def unpack_kernel(dec, sgrad, total0, total1, *refs):
-    outs, staged, totals, sems = refs[:9], refs[9:16], refs[16:18], refs[18]
-    loads = [pltpu.make_async_copy(src, dst, sems.at[9 + i]) for i, (src, dst) in enumerate(zip((total0, total1), totals))]
-    copies = [pltpu.make_async_copy(src, dst, sems.at[i]) for i, (src, dst) in enumerate(zip((dec, sgrad) + staged, outs))]
-    for copy in loads + copies[:2]:
-        copy.start()
+def unpack_kernel(*refs):
+    ins, outs, staged, held, sems = refs[:4], refs[4:13], refs[13:20], refs[20:24], refs[24]
+    loads = [pltpu.make_async_copy(src, dst, sems.at[9 + i]) for i, (src, dst) in enumerate(zip(ins, held))]
+    sources = tuple(held[:2]) + tuple(staged)
+    copies = [pltpu.make_async_copy(src, dst, sems.at[i]) for i, (src, dst) in enumerate(zip(sources, outs))]
+    for i in (2, 3, 0, 1):
+        loads[i].start()
     for b in range(2):
-        loads[b].wait()
-        unpack(b, totals[b], staged)
-    for copy in copies[2:]:
+        loads[2 + b].wait()
+        unpack(b, held[2 + b], staged)
+    for i in range(2):
+        loads[i].wait()
+    for copy in copies:
         copy.start()
     for copy in copies:
         copy.wait()
@@ -495,18 +498,20 @@
         load.wait()
     sig, cot, table = args[0], args[1], args[8]
     unfold(sig, field)
-    unfold(cot, send_cot)
-    for b in range(2):
-        build_bias(table[:, b, :], saved[b].bias)
+    build_bias(table[:, 0, :], saved[0].bias)
     weights = [read_weights(b, args[2:8]) for b in range(2)]
     output = forward(field[...], weights[0], saved[0], None)
     send_out[...] = output.astype(BF16)
 
     pl.semaphore_wait(barrier, greetings)
     out_copies = up_halo(0, send_out)
+    for copy in out_copies:
+        copy.start()
+    unfold(cot, send_cot)
     cot_copies = up_halo(1, send_cot)
-    for copy in out_copies + cot_copies:
+    for copy in cot_copies:
         copy.start()
+    build_bias(table[:, 1, :], saved[1].bias)
     for copy in out_copies:
         copy.wait()
     is_last = (lat == n_lat - 1).astype(jnp.int32)
@@ -534,17 +539,14 @@
         copy.wait()
     factor = 1.0 / math.sqrt(PIX * n_lat * n_lon)
 
-    def early():
-        upper.start()
-        whole.add_plane()
-
-    back = backward(unshifted(3, send_grad), weights[0], saved[0], packs[0], early)
+    back = backward(unshifted(3, send_grad), weights[0], saved[0], packs[0], upper.start)
     lower.start()
     fold(back, fields[1])
     stores[1].start()
-    whole.add_all(factor)
+    whole.add_plane()
     upper.add_plane()
     lower.add_plane()
+    whole.add_all(factor)
     upper.add_all(factor)
     lower.add_all(factor)
     whole.finish()
@@ -597,8 +599,9 @@
             in_specs=[hbm] * 4,
             out_specs=[hbm] * 9,
             scratch_shapes=[pltpu.VMEM(leaf.shape, F32) for leaf in args[2:]]
+            + [pltpu.VMEM(sig.shape, BF16)] * 2
             + [pltpu.VMEM((ROWS, 128), BF16)] * 2
-            + [dma((11,))],
+            + [dma((13,))],
             compiler_params=pltpu.CompilerParams(vmem_limit_bytes=62 * 1024 * 1024),
         )(*results)
         decoded, sgrad, qkv, proj, up, down, gammas, betas, tables = outs

time: 58.9 us -> 53.4 us (0.907)
  Pallas kernels: 58.1 us -> 52.6 us
    pallas_call x1, Pallas kernels: 7.17 us -> 2.51 us  [per_device(): pl.pallas_call(unpack_kernel, out_shape=[field, field] + grads, in_specs=...]
    pallas_call x1, Pallas kernels: 51 us -> 50.1 us  [per_device(): pl.pallas_call(functools.partial(kernel, n_lat, n_lon), out_shape=[field,...]
where the time goes in v3:
time: 53.4 us; the launch traced here: 53.3 us
  Pallas kernels  52.6 us (99%)
  between operations  0.65 us (1%)
    pallas_call x1, Pallas kernels, per_device(): pl.pallas_call(functools.partial(kernel, n_lat, n_lon), out_shape=[field,...  50.1 us
    pallas_call x1, Pallas kernels, per_device(): pl.pallas_call(unpack_kernel, out_shape=[field, field] + grads, in_specs=...  2.51 us

profile of v3, /device:TPU:1, one launch (start us, length us, event | category | flops | bytes accessed | tf_op | source)
XLA Modules:
  0.0 53.3 jit_solution(3835544152046200815)
XLA Ops:
  0.6 50.1 %shard_map.160 = (bf16[8,6144]{1,0:T(8,128)(2,1)}, bf16[8,6144]{1,0:T(8,128)(2,1)}, bf16[1024,128]{1,0:T(8,128)(2,1)}, bf16[1024,128]{1,0:T(8,128)(2,1)}) custom-call(bf16[8,6144]{1,0:T(8,128)(2,1)} %refs_0_.1, bf16[8,6144]{1,0:T(8,128)(2,1)} %refs_1_.1, bf16[2,96,288]{2,1,0:T(8,128)(2,1)} %refs_2_.1, bf16[2,96,96]{2,1,0:T(8,128)(2,1)} %refs_3_.1, ...), custom_call_target="tpu_custom_call" | custom-call | tf_op jit(solution)/shard_map/pallas_call | solution.py:585
  50.8 2.5 %shard_map.161 = (bf16[8,6144]{1,0:T(8,128)(2,1)}, bf16[8,6144]{1,0:T(8,128)(2,1)}, f32[2,96,288]{2,1,0:T(8,128)}, f32[2,96,96]{2,1,0:T(8,128)}, f32[2,96,384]{2...) custom-call(bf16[8,6144]{1,0:T(8,128)(2,1)} %get-tuple-element.22.refs_0_,, ...), custom_call_target="tpu_custom_call" | custom-call | tf_op jit(solution)/shard_map/pallas_call | solution.py:596

commit v4 on v3

--- a/solution.py
+++ b/solution.py
@@ -125,8 +125,8 @@
     return ((query // TOKENS) * 128 + column * 16 + row == place).astype(F32)
 
 
-def build_bias(table, bias):
-    slots = dot_split(table, rel_slots().astype(BF16))
+def build_bias(table, slot_ref, spread_ref, bias):
+    slots = dot_split(table, slot_ref[...])
     sub = iota((8, SLOTS), 0)
     heads = []
     for h in range(HEADS):
@@ -140,7 +140,7 @@
             groups.append(pltpu.roll(skew, turn % SLOTS, 1)[:, :128])
         heads.append(jnp.concatenate(groups, axis=0))
     wide = jnp.concatenate(heads, axis=1)
-    back = spread_queries().astype(BF16)
+    back = spread_ref[...]
     high = wide.astype(BF16)
     rest = wide - high.astype(F32)
     middle = rest.astype(BF16)
@@ -148,8 +148,8 @@
     bias[...] = dot(high, back, (1, 1)) + dot(middle, back, (1, 1)) + dot(low, back, (1, 1))
 
 
-def table_slots(total):
-    wide = dot(total.astype(BF16), spread_queries().astype(BF16))
+def table_slots(total, spread_ref):
+    wide = dot(total.astype(BF16), spread_ref[...])
     sub = iota((8, SLOTS), 0)
     blank = jnp.zeros((8, 128), F32)
     lines = []
@@ -165,37 +165,52 @@
     return lines
 
 
-def forward(x, weights, saved, blocked):
-    (wq, wk, wv), wproj, wup, wdown, gamma, beta = weights
+def gelu_parts(up):
+    square = up * up
+    bent = jnp.tanh(GELU_A * up * (1.0 + GELU_B * square))
+    return square, bent, 0.5 * (1.0 + bent)
+
+
+def gelu_slope(up, square, bent, half):
+    return half + 0.5 * up * (1.0 - bent * bent) * (GELU_A * (1.0 + 3.0 * GELU_B * square))
+
+
+def project(x, weights, saved, start):
+    rows = slice(start, start + x.shape[0])
+    wq, wk, wv = weights[0]
     hat, scale = normalise(x)
-    saved.hat1[...] = hat
-    saved.scale1[...] = scale
+    saved.hat1[rows, :] = hat
+    saved.scale1[rows, :] = scale
     normed = hat.astype(BF16)
-    saved.query[...] = dot(normed, wq).astype(BF16)
-    saved.key[...] = dot(normed, wk).astype(BF16)
-    saved.value[...] = dot(normed, wv).astype(BF16)
+    saved.query[rows, :] = dot(normed, wq).astype(BF16)
+    saved.key[rows, :] = dot(normed, wk).astype(BF16)
+    saved.value[rows, :] = dot(normed, wv).astype(BF16)
+
+
+def forward(x, weights, saved, blocked, slope_later):
+    _, wproj, wup, wdown, gamma, beta = weights
     bias = saved.bias[...]
-    for w in range(WINDOWS):
-        query = stack_heads(window(saved.query, w))
-        score = dot(window(saved.key, w), query, (1, 1)) * (HEAD**-0.5) + bias
-        if blocked is not None:
-            score = jnp.where(blocked, -1e9, score)
-        raised = jnp.exp(score - jnp.max(score, axis=0, keepdims=True))
-        attn = raised / jnp.sum(raised, axis=0, keepdims=True)
-        saved.attn[w] = attn
-        mixed = merge_heads(dot(attn.astype(BF16), window(saved.value, w), (0, 0)))
-        put_window(saved.mixed, w, mixed)
+    every = range(WINDOWS)
+    scores = [dot(window(saved.key, w), stack_heads(window(saved.query, w)), (1, 1)) for w in every]
+    scores = [score * (HEAD**-0.5) + bias for score in scores]
+    if blocked is not None:
+        scores = [jnp.where(blocked, -1e9, score) for score in scores]
+    scores = [jnp.exp(score - jnp.max(score, axis=0, keepdims=True)) for score in scores]
+    attns = [score / jnp.sum(score, axis=0, keepdims=True) for score in scores]
+    for w in every:
+        saved.attn[w] = attns[w]
+    mixed = [dot(attns[w].astype(BF16), window(saved.value, w), (0, 0)) for w in every]
+    for w in every:
+        put_window(saved.mixed, w, merge_heads(mixed[w]))
     hidden = x + dot(saved.mixed[...], wproj)
     hat, scale = normalise(hidden)
     saved.hat2[...] = hat
     saved.scale2[...] = scale
     up = dot(hat.astype(BF16), wup)
-    square = up * up
-    bent = jnp.tanh(GELU_A * up * (1.0 + GELU_B * square))
-    half = 0.5 * (1.0 + bent)
+    square, bent, half = gelu_parts(up)
     lifted = (up * half).astype(BF16)
     saved.lifted[...] = lifted
-    saved.slope[...] = half + 0.5 * up * (1.0 - bent * bent) * (GELU_A * (1.0 + 3.0 * GELU_B * square))
+    saved.slope[...] = up if slope_later else gelu_slope(up, square, bent, half)
     gdn = hidden + dot(lifted, wdown, (1, 1))
     power = beta + dot((gdn * gdn).astype(BF16), gamma)
     root = lax.rsqrt(power)
@@ -204,57 +219,88 @@
     return gdn * root
 
 
-def backward(grad, weights, saved, pack, early=None):
-    (wq, wk, wv), wproj, wup, wdown, gamma, beta = weights
+def prepare(saved):
+    up = saved.slope[...]
+    saved.slope[...] = gelu_slope(up, *gelu_parts(up))
+
+
+def transpose_saved(saved):
+    saved.normed_t[...] = saved.hat1[...].T.astype(BF16)
+    saved.hat2_t[...] = saved.hat2[...].T.astype(BF16)
+    saved.mixed_t[...] = saved.mixed[...].astype(F32).T.astype(BF16)
     gdn = saved.gdn[...]
-    root = saved.root[...]
+    saved.square_t[...] = (gdn * gdn).T.astype(BF16)
+
+
+def back_mlp(grad, weights, saved, start):
+    rows = slice(start, start + grad.shape[0])
+    _, wproj, wup, wdown, gamma, _ = weights
+    gdn = saved.gdn[rows, :]
+    root = saved.root[rows, :]
     dpower = -0.5 * grad * gdn * (root * root * root)
     dpower_16 = dpower.astype(BF16)
-    gamma_grad = dot((gdn * gdn).astype(BF16), dpower_16, (0, 0))
-    for i in range(3):
-        pack[576 + C * i : 576 + C * (i + 1), C:128] = gamma_grad[:, 32 * i : 32 * (i + 1)].astype(BF16)
-    beta_grad = jnp.sum(dpower, axis=0, keepdims=True)
+    saved.dpower[rows, :] = dpower_16
     dgdn = grad * root + 2.0 * gdn * dot(dpower_16, gamma, (1, 1))
     dgdn_16 = dgdn.astype(BF16)
-    down_grad = dot(dgdn_16, saved.lifted[...], (0, 0))
-    for i in range(3):
-        pack[288 + C * i : 288 + C * (i + 1), :] = down_grad[:, 128 * i : 128 * (i + 1)].astype(BF16)
-    dup = (dot(dgdn_16, wdown) * saved.slope[...]).astype(BF16)
-    hat2 = saved.hat2[...]
-    up_grad = dot(hat2.astype(BF16), dup, (0, 0))
+    saved.dgdn[rows, :] = dgdn_16
+    dup = (dot(dgdn_16, wdown) * saved.slope[rows, :]).astype(BF16)
+    saved.dup[rows, :] = dup
+    dhidden = dgdn + norm_back(dot(dup, wup, (1, 1)), saved.hat2[rows, :], saved.scale2[rows, :])
+    dhidden_16 = dhidden.astype(BF16)
+    saved.dhidden[rows, :] = dhidden_16
+    saved.dmixed[rows, :] = dot(dhidden_16, wproj, (1, 1)).astype(BF16)
+    saved.wide[rows, :] = dhidden
+    return jnp.sum(dpower, axis=0, keepdims=True)
+
+
+def grads_mlp(saved, pack):
+    down_grad = dot(saved.dgdn[...], saved.lifted[...], (0, 0))
+    up_grad = dot(saved.hat2_t[...], saved.dup[...])
+    gamma_grad = dot(saved.square_t[...], saved.dpower[...])
     for i in range(3):
         pack[C * i : C * (i + 1), :] = up_grad[:, 128 * i : 128 * (i + 1)].astype(BF16)
-    dhidden = dgdn + norm_back(dot(dup, wup, (1, 1)), hat2, saved.scale2[...])
-    dhidden_16 = dhidden.astype(BF16)
-    proj_grad = dot(saved.mixed[...], dhidden_16, (0, 0))
-    pack[864:960, 0:C] = proj_grad.astype(BF16)
-    saved.dmixed[...] = dot(dhidden_16, wproj, (1, 1)).astype(BF16)
-    if early is not None:
-        early()
-    total = jnp.zeros((TOKENS, HEADS * TOKENS), F32)
-    for w in range(WINDOWS):
-        dmixed = stack_heads(window(saved.dmixed, w))
+        pack[288 + C * i : 288 + C * (i + 1), :] = down_grad[:, 128 * i : 128 * (i + 1)].astype(BF16)
+        pack[576 + C * i : 576 + C * (i + 1), C:128] = gamma_grad[:, 32 * i : 32 * (i + 1)].astype(BF16)
+    pack[864:960, 0:C] = dot(saved.mixed_t[...], saved.dhidden[...]).astype(BF16)
+
+
+def back_attention(saved):
+    every = range(WINDOWS)
+    dmixed = [stack_heads(window(saved.dmixed, w)) for w in every]
+    dattns = [dot(window(saved.value, w), dmixed[w], (1, 1)) for w in every]
+    dvalues = [dot(saved.attn[w].astype(BF16), dmixed[w]) for w in every]
+    for w in every:
+        put_window(saved.dvalue, w, dvalues[w])
+    dscores = []
+    for w in every:
         attn = saved.attn[w]
-        dattn = dot(window(saved.value, w), dmixed, (1, 1))
-        put_window(saved.dvalue, w, dot(attn.astype(BF16), dmixed))
-        dscore = attn * (dattn - jnp.sum(attn * dattn, axis=0, keepdims=True))
-        total = total + dscore
-        dscore = (dscore * (HEAD**-0.5)).astype(BF16)
-        put_window(saved.dkey, w, dot(dscore, stack_heads(window(saved.query, w))))
-        put_window(saved.dquery, w, merge_heads(dot(dscore, window(saved.key, w), (0, 0))))
-    lines = table_slots(total)
-    hat1 = saved.hat1[...]
-    normed = hat1.astype(BF16)
-    dnormed = jnp.zeros((PIX, C), F32)
-    for i, (part, weight) in enumerate(((saved.dquery, wq), (saved.dkey, wk), (saved.dvalue, wv))):
-        piece = part[...]
-        pack[576 + C * i : 576 + C * (i + 1), 0:C] = dot(normed, piece, (0, 0)).astype(BF16)
-        dnormed = dnormed + dot(piece, weight, (1, 1))
+        dscores.append(attn * (dattns[w] - jnp.sum(attn * dattns[w], axis=0, keepdims=True)))
+    total = dscores[0]
+    for w in every[1:]:
+        total = total + dscores[w]
+    dscores = [(dscore * (HEAD**-0.5)).astype(BF16) for dscore in dscores]
+    dqueries = [dot(dscores[w], window(saved.key, w), (0, 0)) for w in every]
+    dkeys = [dot(dscores[w], stack_heads(window(saved.query, w))) for w in every]
+    for w in every:
+        put_window(saved.dkey, w, dkeys[w])
+        put_window(saved.dquery, w, merge_heads(dqueries[w]))
+    return total
+
+
+def grads_attention(saved, pack, total, beta_grad, spread_ref):
+    for i, part in enumerate((saved.dquery, saved.dkey, saved.dvalue)):
+        pack[576 + C * i : 576 + C * (i + 1), 0:C] = dot(saved.normed_t[...], part[...]).astype(BF16)
     edge = jnp.concatenate([beta_grad, jnp.zeros((1, 128 - C), F32)], axis=1)
+    lines = table_slots(total, spread_ref)
     rows = [edge] + [line[:, 128 * i : 128 * (i + 1)] for line in lines for i in range(2)]
     rows.append(jnp.zeros((ROWS - 967, 128), F32))
     pack[960:ROWS, :] = jnp.concatenate(rows, axis=0).astype(BF16)
-    return dhidden + norm_back(dnormed, hat1, saved.scale1[...])
+
+
+def back_input(weights, saved):
+    wq, wk, wv = weights[0]
+    dnormed = dot(saved.dquery[...], wq, (1, 1)) + dot(saved.dkey[...], wk, (1, 1)) + dot(saved.dvalue[...], wv, (1, 1))
+    return saved.wide[...] + norm_back(dnormed, saved.hat1[...], saved.scale1[...])
 
 
 class Saved:
@@ -277,6 +323,15 @@
         "dquery": ((PIX, C), BF16),
         "dkey": ((PIX, C), BF16),
         "dvalue": ((PIX, C), BF16),
+        "dpower": ((PIX, C), BF16),
+        "dgdn": ((PIX, C), BF16),
+        "dup": ((PIX, HID), BF16),
+        "dhidden": ((PIX, C), BF16),
+        "wide": ((PIX, C), F32),
+        "normed_t": ((C, PIX), BF16),
+        "hat2_t": ((C, PIX), BF16),
+        "mixed_t": ((C, PIX), BF16),
+        "square_t": ((C, PIX), BF16),
     }
 
     def __init__(self, refs):
@@ -430,7 +485,7 @@
     hbm_args = take(9)
     results = take(4)
     args = take(9)
-    (arg_sems,) = take(1)
+    arg_sems, slot_ref, spread_ref = take(3)
     saved = [Saved(take(len(Saved.names))) for _ in range(2)]
     field, send_out, send_cot, send_dec, send_grad = take(5)
     south, east, corner, halo_send, halo_recv = take(5)
@@ -494,13 +549,17 @@
         parts = [corner[i], south[i, 0 : HALF - UNIT, :], east[i], ref[0 : HALF - UNIT, :]]
         return jnp.concatenate([part.astype(F32) for part in parts], axis=0)
 
-    for load in loads:
+    sig, cot, table = args[0], args[1], args[8]
+    slot_ref[...] = rel_slots().astype(BF16)
+    spread_ref[...] = spread_queries().astype(BF16)
+    loads[8].wait()
+    build_bias(table[:, 0, :], slot_ref, spread_ref, saved[0].bias)
+    for load in loads[:8]:
         load.wait()
-    sig, cot, table = args[0], args[1], args[8]
     unfold(sig, field)
-    build_bias(table[:, 0, :], saved[0].bias)
     weights = [read_weights(b, args[2:8]) for b in range(2)]
-    output = forward(field[...], weights[0], saved[0], None)
+    project(field[...], weights[0], saved[0], 0)
+    output = forward(field[...], weights[0], saved[0], None, True)
     send_out[...] = output.astype(BF16)
 
     pl.semaphore_wait(barrier, greetings)
@@ -511,37 +570,53 @@
     cot_copies = up_halo(1, send_cot)
     for copy in cot_copies:
         copy.start()
-    build_bias(table[:, 1, :], saved[1].bias)
-    for copy in out_copies:
-        copy.wait()
+    build_bias(table[:, 1, :], slot_ref, spread_ref, saved[1].bias)
     is_last = (lat == n_lat - 1).astype(jnp.int32)
     shape = (TOKENS, HEADS * TOKENS)
     differ = (iota(shape, 0) // 32 != (iota(shape, 1) % TOKENS) // 32).astype(jnp.int32)
     blocked = differ * is_last > 0
-    output = forward(shifted(0, send_out), weights[1], saved[1], blocked)
+    own = HALF - UNIT
+    project(send_out[HALF + UNIT : PIX, :].astype(F32), weights[1], saved[1], 0)
+    prepare(saved[0])
+    for copy in out_copies:
+        copy.wait()
+    field[...] = shifted(0, send_out)
+    project(field[own:PIX, :], weights[1], saved[1], own)
+    output = forward(field[...], weights[1], saved[1], blocked, False)
     send_dec[...] = output.astype(BF16)
     dec_copies = down_halo(2, send_dec)
     for copy in dec_copies:
         copy.start()
     for copy in cot_copies:
         copy.wait()
-    back = backward(shifted(1, send_cot), weights[1], saved[1], packs[1])
-    send_grad[...] = back.astype(BF16)
+    beta_grad = back_mlp(shifted(1, send_cot), weights[1], saved[1], 0)
+    total = back_attention(saved[1])
+    send_grad[...] = back_input(weights[1], saved[1]).astype(BF16)
     grad_copies = down_halo(3, send_grad)
     for copy in grad_copies:
         copy.start()
+    transpose_saved(saved[1])
+    grads_mlp(saved[1], packs[1])
+    grads_attention(saved[1], packs[1], total, beta_grad, spread_ref)
     whole.start()
     for copy in dec_copies:
         copy.wait()
     fold(unshifted(2, send_dec), fields[0])
     stores[0].start()
+    transpose_saved(saved[0])
+    beta_grad = back_mlp(send_grad[0:own, :].astype(F32), weights[0], saved[0], PIX - own)
     for copy in grad_copies:
         copy.wait()
     factor = 1.0 / math.sqrt(PIX * n_lat * n_lon)
 
-    back = backward(unshifted(3, send_grad), weights[0], saved[0], packs[0], upper.start)
+    field[...] = unshifted(3, send_grad)
+    beta_grad = beta_grad + back_mlp(field[0 : PIX - own, :], weights[0], saved[0], 0)
+    grads_mlp(saved[0], packs[0])
+    upper.start()
+    total = back_attention(saved[0])
+    grads_attention(saved[0], packs[0], total, beta_grad, spread_ref)
     lower.start()
-    fold(back, fields[1])
+    fold(back_input(weights[0], saved[0]), fields[1])
     stores[1].start()
     whole.add_plane()
     upper.add_plane()
@@ -566,6 +641,7 @@
         args = (sig, cot, wqkv, wproj, wup, jnp.swapaxes(wdown, 1, 2), gamma, beta, jnp.swapaxes(table, 0, 1))
         saved = [pltpu.VMEM(shape, kind) for shape, kind in Saved.names.values()]
         scratch = [pltpu.VMEM(arg.shape, arg.dtype) for arg in args] + [dma((9,))]
+        scratch += [pltpu.VMEM((RELS, SLOTS), BF16), pltpu.VMEM((HEADS * TOKENS, HEADS * 128), BF16)]
         scratch += saved + saved
         scratch += [pltpu.VMEM((PIX, C), F32)] + [pltpu.VMEM((PIX, C), BF16)] * 4
         scratch += [

time: 53.4 us -> 48 us (0.90)
  Pallas kernels: 52.6 us -> 47.3 us
    pallas_call x1, Pallas kernels: 50.1 us -> 44.8 us  [per_device(): pl.pallas_call(functools.partial(kernel, n_lat, n_lon), out_shape=[field,...]
where the time goes in v4:
time: 48 us; the launch traced here: 47.9 us
  Pallas kernels  47.3 us (99%)
  between operations  0.65 us (1%)
    pallas_call x1, Pallas kernels, per_device(): pl.pallas_call(functools.partial(kernel, n_lat, n_lon), out_shape=[field,...  44.8 us
    pallas_call x1, Pallas kernels, per_device(): pl.pallas_call(unpack_kernel, out_shape=[field, field] + grads, in_specs=...  2.51 us

profile of v4, /device:TPU:1, one launch (start us, length us, event | category | flops | bytes accessed | tf_op | source)
XLA Modules:
  0.0 47.9 jit_solution(13240966588378525718)
XLA Ops:
  0.6 44.8 %shard_map.160 = (bf16[8,6144]{1,0:T(8,128)(2,1)}, bf16[8,6144]{1,0:T(8,128)(2,1)}, bf16[1024,128]{1,0:T(8,128)(2,1)}, bf16[1024,128]{1,0:T(8,128)(2,1)}) custom-call(bf16[8,6144]{1,0:T(8,128)(2,1)} %refs_0_.1, bf16[8,6144]{1,0:T(8,128)(2,1)} %refs_1_.1, bf16[2,96,288]{2,1,0:T(8,128)(2,1)} %refs_2_.1, bf16[2,96,96]{2,1,0:T(8,128)(2,1)} %refs_3_.1, ...), custom_call_target="tpu_custom_call" | custom-call | tf_op jit(solution)/shard_map/pallas_call | solution.py:661
  45.4 2.5 %shard_map.161 = (bf16[8,6144]{1,0:T(8,128)(2,1)}, bf16[8,6144]{1,0:T(8,128)(2,1)}, f32[2,96,288]{2,1,0:T(8,128)}, f32[2,96,96]{2,1,0:T(8,128)}, f32[2,96,384]{2...) custom-call(bf16[8,6144]{1,0:T(8,128)(2,1)} %get-tuple-element.22.refs_0_,, ...), custom_call_target="tpu_custom_call" | custom-call | tf_op jit(solution)/shard_map/pallas_call | solution.py:672

commit v5 on v4

--- a/solution.py
+++ b/solution.py
@@ -353,14 +353,24 @@
 
 
 class Exchange:
-    def __init__(self, n_lat, n_lon, base, pack, total, first, planes, sems):
-        self.n_lat, self.planes_n, self.size = n_lat, n_lon // QUAD, n_lat * QUAD
+    width = QUAD
+    turns = (2, 1, 3, 0)
+
+    def __init__(self, n_lat, n_lon, base, pack, total, first, planes, mine, sems):
+        self.n_lat, self.planes_n, self.size = n_lat, n_lon // QUAD, n_lat * self.width
+        self.lat, self.lon = lax.axis_index("lat"), lax.axis_index("lon")
+        self.z = self.lon // QUAD
+        self.quad = self.column(self.lon)
         self.base, self.pack, self.total = base, pack, total
-        self.first, self.planes, self.sems = first, planes, sems
+        self.first, self.planes, self.mine, self.sems = first, planes, mine, sems
         self.rows = first.shape[1]
-        self.lat, lon = lax.axis_index("lat"), lax.axis_index("lon")
-        self.quad, self.z = lax.rem(lon, QUAD), lon // QUAD
-        self.place = self.lat * QUAD + self.quad
+        self.place = self.lat * self.width + self.quad
+
+    def column(self, lon):
+        return lax.rem(lon, QUAD)
+
+    def device_of(self, lat, quad):
+        return (lat, self.z * QUAD + quad)
 
     def piece(self, ref, i):
         return ref.at[pl.ds(pl.multiple_of(self.base + i * self.rows, UNIT), self.rows), :]
@@ -368,33 +378,34 @@
     def in_plane(self, make):
         def body(i, _):
             step = lax.rem(4 * i + 1, 7) + 1 if self.n_lat == 8 else i + 1
-            for turn in (2, 1, 3, 0):
+            for turn in self.turns:
                 make(step, turn).start()
             return 0
 
         lax.fori_loop(0, self.n_lat - 1, body, 0)
-        for turn in (2, 1, 3):
+        for turn in self.turns[:-1]:
             make(0, turn).start()
 
     def target(self, step, turn):
         lat = lax.rem(self.lat + step, self.n_lat)
-        quad = lax.rem(self.quad + turn, QUAD)
-        return lat * QUAD + quad, (lat, self.z * QUAD + quad)
+        quad = lax.rem(self.quad + turn, self.width)
+        return lat * self.width + quad, self.device_of(lat, quad)
 
     def scatter_copy(self, step, turn):
         place, device = self.target(step, turn)
-        slot = self.first.at[step * QUAD + turn]
+        slot = self.first.at[step * self.width + turn]
         return copy_to(self.piece(self.pack, place), slot, self.sems.at[0], self.sems.at[1], device)
 
     def gather_copy(self, step, turn):
         _, device = self.target(step, turn)
-        mine = self.piece(self.total, self.place)
-        return copy_to(mine, mine, self.sems.at[4], self.sems.at[5], device)
+        return copy_to(self.mine, self.piece(self.total, self.place), self.sems.at[4], self.sems.at[5], device)
+
+    def own_copy(self):
+        return pltpu.make_async_copy(self.mine, self.piece(self.total, self.place), self.sems.at[6])
 
     def plane_copy(self, step):
-        z = lax.rem(self.z + step, self.planes_n)
         slot = self.planes.at[self.z]
-        device = (self.lat, z * QUAD + self.quad)
+        device = (self.lat, lax.rem(self.lon + step * QUAD, self.planes_n * QUAD))
         return copy_to(slot, slot, self.sems.at[2], self.sems.at[3], device)
 
     def wait_both(self, ref, sem):
@@ -423,19 +434,66 @@
         total = self.planes[0].astype(F32)
         for i in range(1, self.planes_n):
             total = total + self.planes[i].astype(F32)
-        self.piece(self.total, self.place)[...] = (total * factor).astype(BF16)
+        self.mine[...] = (total * factor).astype(BF16)
         self.in_plane(self.gather_copy)
+        self.own_copy().start()
 
     def finish(self):
-        self.wait_both(self.total.at[pl.ds(self.base, (self.size - 1) * self.rows), :], 4)
-
-
-def exchange_scratch(n_lat, n_lon, rows):
-    rows = rows // (n_lat * QUAD)
+        self.wait_both(self.total.at[pl.ds(0, (self.size - 1) * self.rows), :], 4)
+        self.own_copy().wait()
+
+
+class PairedExchange(Exchange):
+    width = QUAD // 2
+    turns = (1, 0)
+
+    def __init__(self, n_lat, n_lon, pack, total, half, first, planes, mine, sems):
+        self.half = half
+        self.core = lax.rem(lax.axis_index("lon"), 2)
+        super().__init__(n_lat, n_lon, self.core * (ROWS // 2), pack, total, first, planes, mine, sems)
+
+    def column(self, lon):
+        return lax.rem(lon, QUAD) // 2
+
+    def device_of(self, lat, quad):
+        return (lat, self.z * QUAD + quad * 2 + self.core)
+
+    def half_of(self, ref, core):
+        return ref.at[pl.ds(pl.multiple_of(core * (ROWS // 2), ROWS // 2), ROWS // 2), :]
+
+    def pair_copy(self):
+        device = (self.lat, self.lon + 1 - 2 * self.core)
+        return copy_to(self.half_of(self.pack, 1 - self.core), self.half, self.sems.at[7], self.sems.at[8], device)
+
+    def swap_copy(self):
+        device = (self.lat, self.lon + 1 - 2 * self.core)
+        mine = self.half_of(self.total, self.core)
+        return copy_to(mine, mine, self.sems.at[9], self.sems.at[10], device)
+
+    def start_pair(self):
+        self.pair_copy().start()
+
+    def add_pair(self):
+        self.pair_copy().wait()
+        mine = self.half_of(self.pack, self.core)
+        mine[...] = (mine[...].astype(F32) + self.half[...].astype(F32)).astype(BF16)
+        self.start()
+
+    def swap(self):
+        super().finish()
+        self.swap_copy().start()
+
+    def finish(self):
+        self.swap_copy().wait()
+
+
+def exchange_scratch(n_lat, n_lon, rows, members):
+    rows = rows // members
     return [
-        pltpu.VMEM((n_lat * QUAD, rows, 128), BF16),
+        pltpu.VMEM((members, rows, 128), BF16),
         pltpu.VMEM((n_lon // QUAD, rows, 128), BF16),
-        pltpu.SemaphoreType.DMA((6,)),
+        pltpu.VMEM((rows, 128), BF16),
+        pltpu.SemaphoreType.DMA((11,)),
     ]
 
 
@@ -489,17 +547,18 @@
     saved = [Saved(take(len(Saved.names))) for _ in range(2)]
     field, send_out, send_cot, send_dec, send_grad = take(5)
     south, east, corner, halo_send, halo_recv = take(5)
-    packs, fields, totals = take(2), take(2), take(2)
+    packs, fields = take(2), take(2)
+    (staged,) = take(1)
     (result_sems,) = take(1)
-    whole = Exchange(n_lat, n_lon, 0, packs[1], totals[1], *take(3))
-    upper = Exchange(n_lat, n_lon, 0, packs[0], totals[0], *take(3))
-    lower = Exchange(n_lat, n_lon, ROWS // 2, packs[0], totals[0], *take(3))
+    whole = PairedExchange(n_lat, n_lon, packs[1], staged, *take(5))
+    upper = Exchange(n_lat, n_lon, 0, packs[0], results[2], *take(4))
+    lower = Exchange(n_lat, n_lon, ROWS // 2, packs[0], results[2], *take(4))
     lat, lon = lax.axis_index("lat"), lax.axis_index("lon")
     above, below = lax.rem(lat + n_lat - 1, n_lat), lax.rem(lat + 1, n_lat)
     west, easterly = lax.rem(lon + n_lon - 1, n_lon), lax.rem(lon + 1, n_lon)
 
     stores = [
-        pltpu.make_async_copy(src, dst, result_sems.at[i]) for i, (src, dst) in enumerate(zip(fields + totals, results))
+        pltpu.make_async_copy(src, dst, result_sems.at[i]) for i, (src, dst) in enumerate(zip(fields + [staged], results[:2] + results[3:]))
     ]
     loads = [pltpu.make_async_copy(src, dst, arg_sems.at[i]) for i, (src, dst) in enumerate(zip(hbm_args, args))]
     for load in loads:
@@ -510,7 +569,7 @@
         pl.semaphore_signal(barrier, inc=1, device_id=device, device_id_type=MESH)
 
     def greet_plane(i, _):
-        _, device = whole.target(i // QUAD, lax.rem(i, QUAD))
+        _, device = upper.target(i // QUAD, lax.rem(i, QUAD))
         greet(device)
         return 0
 
@@ -557,7 +616,7 @@
     for load in loads[:8]:
         load.wait()
     unfold(sig, field)
-    weights = [read_weights(b, args[2:8]) for b in range(2)]
+    weights = [read_weights(0, args[2:8])]
     project(field[...], weights[0], saved[0], 0)
     output = forward(field[...], weights[0], saved[0], None, True)
     send_out[...] = output.astype(BF16)
@@ -575,6 +634,7 @@
     shape = (TOKENS, HEADS * TOKENS)
     differ = (iota(shape, 0) // 32 != (iota(shape, 1) % TOKENS) // 32).astype(jnp.int32)
     blocked = differ * is_last > 0
+    weights.append(read_weights(1, args[2:8]))
     own = HALF - UNIT
     project(send_out[HALF + UNIT : PIX, :].astype(F32), weights[1], saved[1], 0)
     prepare(saved[0])
@@ -598,13 +658,14 @@
     transpose_saved(saved[1])
     grads_mlp(saved[1], packs[1])
     grads_attention(saved[1], packs[1], total, beta_grad, spread_ref)
-    whole.start()
+    whole.start_pair()
     for copy in dec_copies:
         copy.wait()
     fold(unshifted(2, send_dec), fields[0])
     stores[0].start()
     transpose_saved(saved[0])
     beta_grad = back_mlp(send_grad[0:own, :].astype(F32), weights[0], saved[0], PIX - own)
+    whole.add_pair()
     for copy in grad_copies:
         copy.wait()
     factor = 1.0 / math.sqrt(PIX * n_lat * n_lon)
@@ -624,11 +685,11 @@
     whole.add_all(factor)
     upper.add_all(factor)
     lower.add_all(factor)
+    whole.swap()
+    upper.finish()
     whole.finish()
-    stores[3].start()
-    upper.finish()
+    stores[2].start()
     lower.finish()
-    stores[2].start()
     for store in stores:
         store.wait()
 
@@ -652,9 +713,10 @@
             dma((12,)),
         ]
         scratch += [pltpu.VMEM((ROWS, 128), BF16)] * 2 + [pltpu.VMEM(sig.shape, BF16)] * 2
-        scratch += [pltpu.VMEM((ROWS, 128), BF16)] * 2 + [dma((4,))]
-        scratch += exchange_scratch(n_lat, n_lon, ROWS)
-        scratch += exchange_scratch(n_lat, n_lon, ROWS // 2) * 2
+        scratch += [pltpu.VMEM((ROWS, 128), BF16), dma((3,))]
+        scratch += [pltpu.VMEM((ROWS // 2, 128), BF16)]
+        scratch += exchange_scratch(n_lat, n_lon, ROWS // 2, n_lat * QUAD // 2)
+        scratch += exchange_scratch(n_lat, n_lon, ROWS // 2, n_lat * QUAD) * 2
         hbm = pl.BlockSpec(memory_space=pltpu.HBM)
         field = jax.ShapeDtypeStruct(sig.shape, BF16)
         total = jax.ShapeDtypeStruct((ROWS, 128), BF16)

time: 48 us -> 46.5 us (0.969)
  Pallas kernels: 47.3 us -> 45.7 us
    pallas_call x1, Pallas kernels: 44.8 us -> 43.2 us  [per_device(): pl.pallas_call(functools.partial(kernel, n_lat, n_lon), out_shape=[field,...]
where the time goes in v5:
time: 46.5 us; the launch traced here: 46.4 us
  Pallas kernels  45.7 us (98%)
  between operations  0.65 us (1%)
    pallas_call x1, Pallas kernels, per_device(): pl.pallas_call(functools.partial(kernel, n_lat, n_lon), out_shape=[field,...  43.2 us
    pallas_call x1, Pallas kernels, per_device(): pl.pallas_call(unpack_kernel, out_shape=[field, field] + grads, in_specs=...  2.51 us

profile of v5, /device:TPU:1, one launch (start us, length us, event | category | flops | bytes accessed | tf_op | source)
XLA Modules:
  0.0 46.4 jit_solution(2030043283056330894)
XLA Ops:
  0.6 43.2 %shard_map.160 = (bf16[8,6144]{1,0:T(8,128)(2,1)}, bf16[8,6144]{1,0:T(8,128)(2,1)}, bf16[1024,128]{1,0:T(8,128)(2,1)}, bf16[1024,128]{1,0:T(8,128)(2,1)}) custom-call(bf16[8,6144]{1,0:T(8,128)(2,1)} %refs_0_.1, bf16[8,6144]{1,0:T(8,128)(2,1)} %refs_1_.1, bf16[2,96,288]{2,1,0:T(8,128)(2,1)} %refs_2_.1, bf16[2,96,96]{2,1,0:T(8,128)(2,1)} %refs_3_.1, ...), custom_call_target="tpu_custom_call" | custom-call | tf_op jit(solution)/shard_map/pallas_call | solution.py:723
  43.9 2.5 %shard_map.161 = (bf16[8,6144]{1,0:T(8,128)(2,1)}, bf16[8,6144]{1,0:T(8,128)(2,1)}, f32[2,96,288]{2,1,0:T(8,128)}, f32[2,96,96]{2,1,0:T(8,128)}, f32[2,96,384]{2...) custom-call(bf16[8,6144]{1,0:T(8,128)(2,1)} %get-tuple-element.22.refs_0_,, ...), custom_call_target="tpu_custom_call" | custom-call | tf_op jit(solution)/shard_map/pallas_call | solution.py:734

commit v6 on v5

--- a/solution.py
+++ b/solution.py
@@ -376,13 +376,10 @@
         return ref.at[pl.ds(pl.multiple_of(self.base + i * self.rows, UNIT), self.rows), :]
 
     def in_plane(self, make):
-        def body(i, _):
-            step = lax.rem(4 * i + 1, 7) + 1 if self.n_lat == 8 else i + 1
+        for i in range(self.n_lat - 1):
+            step = (4 * i + 1) % 7 + 1 if self.n_lat == 8 else i + 1
             for turn in self.turns:
                 make(step, turn).start()
-            return 0
-
-        lax.fori_loop(0, self.n_lat - 1, body, 0)
         for turn in self.turns[:-1]:
             make(0, turn).start()
 
@@ -516,18 +513,24 @@
 
 def unpack_kernel(*refs):
     ins, outs, staged, held, sems = refs[:4], refs[4:13], refs[13:20], refs[20:24], refs[24]
-    loads = [pltpu.make_async_copy(src, dst, sems.at[9 + i]) for i, (src, dst) in enumerate(zip(ins, held))]
-    sources = tuple(held[:2]) + tuple(staged)
-    copies = [pltpu.make_async_copy(src, dst, sems.at[i]) for i, (src, dst) in enumerate(zip(sources, outs))]
-    for i in (2, 3, 0, 1):
+    loads = [pltpu.make_async_copy(src, dst, sems.at[i]) for i, (src, dst) in enumerate(zip(ins, held))]
+    for i in (3, 2, 0, 1):
         loads[i].start()
-    for b in range(2):
+    copies = []
+
+    def store(src, dst):
+        copies.append(pltpu.make_async_copy(src, dst, sems.at[4 + len(copies)]))
+        copies[-1].start()
+
+    for b in (1, 0):
         loads[2 + b].wait()
         unpack(b, held[2 + b], staged)
-    for i in range(2):
-        loads[i].wait()
-    for copy in copies:
-        copy.start()
+        for src, dst in zip(staged[:5], outs[2:7]):
+            store(src.at[b], dst.at[b])
+        loads[b].wait()
+        store(held[b], outs[b])
+    for src, dst in zip(staged[5:], outs[7:]):
+        store(src, dst)
     for copy in copies:
         copy.wait()
 
@@ -739,7 +742,7 @@
             scratch_shapes=[pltpu.VMEM(leaf.shape, F32) for leaf in args[2:]]
             + [pltpu.VMEM(sig.shape, BF16)] * 2
             + [pltpu.VMEM((ROWS, 128), BF16)] * 2
-            + [dma((13,))],
+            + [dma((18,))],
             compiler_params=pltpu.CompilerParams(vmem_limit_bytes=62 * 1024 * 1024),
         )(*results)
         decoded, sgrad, qkv, proj, up, down, gammas, betas, tables = outs

time: 46.5 us -> 46.1 us (level)
  no operation moved by 1% of the time
where the time goes in v6:
time: 46.1 us; the launch traced here: 46 us
  Pallas kernels  45.3 us (98%)
  between operations  0.65 us (1%)
    pallas_call x1, Pallas kernels, per_device(): pl.pallas_call(functools.partial(kernel, n_lat, n_lon), out_shape=[field,...  43 us
    pallas_call x1, Pallas kernels, per_device(): pl.pallas_call(unpack_kernel, out_shape=[field, field] + grads, in_specs=...  2.3 us

profile of v6, /device:TPU:1, one launch (start us, length us, event | category | flops | bytes accessed | tf_op | source)
XLA Modules:
  0.0 46.0 jit_solution(8873231993580230103)
XLA Ops:
  0.6 43.0 %shard_map.160 = (bf16[8,6144]{1,0:T(8,128)(2,1)}, bf16[8,6144]{1,0:T(8,128)(2,1)}, bf16[1024,128]{1,0:T(8,128)(2,1)}, bf16[1024,128]{1,0:T(8,128)(2,1)}) custom-call(bf16[8,6144]{1,0:T(8,128)(2,1)} %refs_0_.1, bf16[8,6144]{1,0:T(8,128)(2,1)} %refs_1_.1, bf16[2,96,288]{2,1,0:T(8,128)(2,1)} %refs_2_.1, bf16[2,96,96]{2,1,0:T(8,128)(2,1)} %refs_3_.1, ...), custom_call_target="tpu_custom_call" | custom-call | tf_op jit(solution)/shard_map/pallas_call | solution.py:726
  43.7 2.3 %shard_map.161 = (bf16[8,6144]{1,0:T(8,128)(2,1)}, bf16[8,6144]{1,0:T(8,128)(2,1)}, f32[2,96,288]{2,1,0:T(8,128)}, f32[2,96,96]{2,1,0:T(8,128)}, f32[2,96,384]{2...) custom-call(bf16[8,6144]{1,0:T(8,128)(2,1)} %get-tuple-element.22.refs_0_,, ...), custom_call_target="tpu_custom_call" | custom-call | tf_op jit(solution)/shard_map/pallas_call | solution.py:737
